TPU v7x, 256 devices: a whole 4x4x8 slice. The times are simulated.
256 devices in a mesh: rep: 32 (over x, z), tp: 8 (over y, core).
Axes of the slice: x: 4, y: 4, z: 8, core: 2. Of those that a mesh axis runs over, the one named last changes fastest.
Arguments:
- res_state: bfloat16 [128, 128, 64, 128], P('rep', 'tp'), may hold values from -0.59765625 to 0.59765625
- res_conv_x: bfloat16 [128, 3, 8192], P('rep', None, 'tp'), may hold values from -6 to 6
- res_conv_bc: bfloat16 [128, 3, 2, 1024], P('rep', None, None, 'tp'), may hold values from -6 to 6
- res_x: bfloat16 [128, 64, 8192], P('rep', None, 'tp'), may hold values from -6 to 6
- res_bc: bfloat16 [128, 64, 2, 1024], P('rep', None, None, 'tp'), may hold values from -6 to 6
- res_z: bfloat16 [128, 64, 8192], P('rep', None, 'tp'), may hold values from -6 to 6
- res_dt: bfloat16 [128, 64, 128], P('rep', None, 'tp'), may hold values from -3 to 3
- res_count: int32 [32], P('rep'), may hold values from 1 to 4, as said below
- hand_state: bfloat16 [32, 128, 64, 128], P('rep', 'tp'), may hold values from -0.59765625 to 0.59765625
- hand_conv_x: bfloat16 [32, 3, 8192], P('rep', None, 'tp'), may hold values from -6 to 6
- hand_conv_bc: bfloat16 [32, 3, 2, 1024], P('rep', None, None, 'tp'), may hold values from -6 to 6
- slot_x: bfloat16 [96, 64, 8192], P('rep', None, 'tp'), may hold values from -6 to 6
- slot_bc: bfloat16 [96, 64, 2, 1024], P('rep', None, None, 'tp'), may hold values from -6 to 6
- slot_z: bfloat16 [96, 64, 8192], P('rep', None, 'tp'), may hold values from -6 to 6
- slot_dt: bfloat16 [96, 64, 128], P('rep', None, 'tp'), may hold values from -3 to 3
- assignment: int32 [32], replicated, may hold values from 0 to 31, as said below
- conv_wx: float32 [4, 8192], P(None, 'tp'), may hold values from -3 to 3
- conv_wbc: float32 [4, 2, 1024], P(None, None, 'tp'), may hold values from -3 to 3
- dt_bias: float32 [128], P('tp'), may hold values from -3 to 0.5
- a_log: float32 [128], P('tp'), may hold values from -2 to 1.2
- d_skip: float32 [128], P('tp'), may hold values from 0.5 to 1.5
- norm_w: float32 [8192], P('tp'), may hold values from 0.5 to 1.5
- out_w: bfloat16 [8192, 4096], P('tp'), may hold values from -0.0625 to 0.0625
Outputs:
- res_out: bfloat16 [128, 64, 4096], P('rep', None, 'tp')
- slot_out: bfloat16 [96, 64, 4096], P('rep', None, 'tp')
- slot_state: bfloat16 [96, 128, 64, 128], P('rep', 'tp')
Inputs may be any that keep to these rules, and one draw needn't show every extreme that they name: `assignment`: request r's handed state starts on replica index r. Each replica receives at most 3 requests and some replica exactly 3. Slot j of a replica serves its j-th request in order of r; inputs of its unused slots are ignored. `res_count`: resident slots j >= the replica's count are spare and give zeros; some replica has exactly 4.
All inputs are finite; a program needn't handle non-finite values.
Results may differ from a plain program's by a relative error of at most 0.019.
Values may be sent and summed in bfloat16 or wider, within the bound.
No kernel may reach another device: no remote copies, remote signals or barrier semaphores. Data moves between devices by JAX's collectives and lax.ppermute only.
A program may use at most 128 MiB of HBM per device.

v0:
```python
import jax
import jax.numpy as jnp
from jax import lax
from jax.sharding import PartitionSpec as P

STEPS = 2
BLOCK = 32
CAP = 3


def decode_request(
    hold_state,
    conv_rows,
    conv_pairs,
    input_x,
    input_pairs,
    input_gate,
    input_step,
    conv_wx,
    conv_wbc,
    dt_bias,
    a_log,
    d_skip,
    norm_w,
    step_count,
    block_rows,
):
    head_count, head_dim, width_state = hold_state.shape
    inner_width = conv_rows.shape[-1]
    groups = conv_pairs.shape[-1] // width_state
    per_group = head_count // groups
    kernel = conv_wx.shape[0]
    highest = lax.Precision.HIGHEST
    decay_rate = -jnp.exp(a_log)
    carried = hold_state.astype(jnp.float32)
    positions = jnp.arange(block_rows)
    causal = (positions[:, None] >= positions[None, :])[:, :, None]
    normed_rows = []
    for step_index in range(step_count):
        first_row = step_index * block_rows
        window_x = jnp.concatenate([conv_rows, input_x[first_row : first_row + block_rows]], 0)
        window_pairs = jnp.concatenate(
            [conv_pairs, input_pairs[first_row : first_row + block_rows]], 0
        )
        conv_rows = window_x[block_rows:]
        conv_pairs = window_pairs[block_rows:]
        summed_x = window_x[0:block_rows].astype(jnp.float32) * conv_wx[0]
        summed_pairs = window_pairs[0:block_rows].astype(jnp.float32) * conv_wbc[0]
        for offset in range(1, kernel):
            summed_x = (
                summed_x
                + window_x[offset : offset + block_rows].astype(jnp.float32) * conv_wx[offset]
            )
            summed_pairs = (
                summed_pairs
                + window_pairs[offset : offset + block_rows].astype(jnp.float32) * conv_wbc[offset]
            )
        x_conv = jax.nn.silu(summed_x).reshape(block_rows, groups, per_group, head_dim)
        pairs_conv = jax.nn.silu(summed_pairs)
        coeff_b = pairs_conv[:, 0].reshape(block_rows, groups, width_state)
        coeff_c = pairs_conv[:, 1].reshape(block_rows, groups, width_state)
        step_size = jax.nn.softplus(
            input_step[first_row : first_row + block_rows].astype(jnp.float32) + dt_bias
        )
        cum_decay = jnp.cumsum(step_size * decay_rate, axis=0)
        difference = cum_decay[:, None, :] - cum_decay[None, :, :]
        decay_mask = jnp.where(causal, jnp.exp(jnp.where(causal, difference, 0.0)), 0.0)
        scores = jnp.einsum("tgn,sgn->tsg", coeff_c, coeff_b, precision=highest)
        weights = (
            decay_mask.reshape(block_rows, block_rows, groups, per_group)
            * scores[..., None]
            * step_size.reshape(1, block_rows, groups, per_group)
        )
        y_inner = jnp.einsum("tsgq,sgqp->tgqp", weights, x_conv, precision=highest)
        grouped = carried.reshape(groups, per_group, head_dim, width_state)
        y_state = (
            jnp.einsum("tgn,gqpn->tgqp", coeff_c, grouped, precision=highest)
            * jnp.exp(cum_decay).reshape(block_rows, groups, per_group)[..., None]
        )
        output = y_inner + y_state + d_skip.reshape(groups, per_group)[None, :, :, None] * x_conv
        tail_weight = (jnp.exp(cum_decay[-1][None, :] - cum_decay) * step_size).reshape(
            block_rows, groups, per_group
        )
        update = jnp.einsum("sgq,sgqp,sgn->gqpn", tail_weight, x_conv, coeff_b, precision=highest)
        carried = carried * jnp.exp(cum_decay[-1])[:, None, None] + update.reshape(
            head_count, head_dim, width_state
        )
        gated = output.reshape(block_rows, inner_width) * jax.nn.silu(
            input_gate[first_row : first_row + block_rows].astype(jnp.float32)
        )
        gated = gated.reshape(block_rows, groups, inner_width // groups)
        mean_square = jnp.mean(gated * gated, axis=-1, keepdims=True)
        normed = (gated * lax.rsqrt(mean_square + 1e-05)).reshape(block_rows, inner_width) * norm_w
        normed_rows.append(normed.astype(jnp.bfloat16))
    return (jnp.concatenate(normed_rows, 0), carried.astype(jnp.bfloat16))


def mask_slots(slot_valid, values_array):
    shaped = slot_valid.reshape((-1,) + (1,) * (values_array.ndim - 1))
    return jnp.where(shaped, values_array, jnp.zeros_like(values_array))


def on_device(
    res_state,
    res_conv_x,
    res_conv_bc,
    res_x,
    res_bc,
    res_z,
    res_dt,
    res_count,
    hand_state,
    hand_conv_x,
    hand_conv_bc,
    slot_x,
    slot_bc,
    slot_z,
    slot_dt,
    assignment,
    conv_wx,
    conv_wbc,
    dt_bias,
    a_log,
    d_skip,
    norm_w,
    out_w,
):
    params = (conv_wx, conv_wbc, dt_bias, a_log, d_skip, norm_w)

    def run_one(*request_item):
        return decode_request(*request_item, *params, STEPS, BLOCK)

    batched = jax.vmap(run_one)
    res_normed, _ = batched(res_state, res_conv_x, res_conv_bc, res_x, res_bc, res_z, res_dt)
    own_index = lax.axis_index("rep")
    replicas = lax.axis_size("rep")
    assigned_here = assignment == own_index
    slot_order = jnp.cumsum(assigned_here.astype(jnp.int32)) - 1
    slot_picks = assigned_here[None, :] & (slot_order[None, :] == jnp.arange(CAP)[:, None])
    sources = jnp.sum(jnp.where(slot_picks, jnp.arange(replicas)[None, :], 0), axis=1)
    slot_valid = jnp.any(slot_picks, axis=1)
    target = jnp.take(assignment, own_index)

    def place_row(values_array):
        empty = jnp.zeros((replicas,) + values_array.shape[1:], values_array.dtype)
        return lax.dynamic_update_slice_in_dim(empty, values_array, target, 0)

    arrived = (
        lax.all_to_all(place_row(hand_state), "rep", split_axis=0, concat_axis=0, tiled=True),
        lax.all_to_all(place_row(hand_conv_x), "rep", split_axis=0, concat_axis=0, tiled=True),
        lax.all_to_all(place_row(hand_conv_bc), "rep", split_axis=0, concat_axis=0, tiled=True),
    )
    slot_init = tuple(
        (
            mask_slots(slot_valid, jnp.take(values_array, sources, axis=0))
            for values_array in arrived
        )
    )
    slot_normed, slot_final = batched(
        slot_init[0], slot_init[1], slot_init[2], slot_x, slot_bc, slot_z, slot_dt
    )
    joined = jnp.concatenate([res_normed, slot_normed], 0)
    partial_sum = jnp.dot(
        joined.reshape(-1, joined.shape[-1]), out_w, preferred_element_type=jnp.float32
    )
    summed = lax.psum_scatter(
        partial_sum.astype(jnp.bfloat16), "tp", scatter_dimension=1, tiled=True
    ).astype(jnp.float32)
    summed = summed.reshape(joined.shape[0], joined.shape[1], summed.shape[-1])
    resident_slots = res_normed.shape[0]
    live_rows = jnp.arange(resident_slots) < res_count[0]
    res_out = jnp.where(live_rows[:, None, None], summed[:resident_slots], 0.0).astype(jnp.bfloat16)
    slot_out = jnp.where(slot_valid[:, None, None], summed[resident_slots:], 0.0).astype(
        jnp.bfloat16
    )
    slot_state = mask_slots(slot_valid, slot_final)
    return (res_out, slot_out, slot_state)


def solution(mesh):
    return jax.shard_map(
        on_device,
        mesh=mesh,
        in_specs=(
            P("rep", "tp", None, None),
            P("rep", None, "tp"),
            P("rep", None, None, "tp"),
            P("rep", None, "tp"),
            P("rep", None, None, "tp"),
            P("rep", None, "tp"),
            P("rep", None, "tp"),
            P("rep"),
            P("rep", "tp", None, None),
            P("rep", None, "tp"),
            P("rep", None, None, "tp"),
            P("rep", None, "tp"),
            P("rep", None, None, "tp"),
            P("rep", None, "tp"),
            P("rep", None, "tp"),
            P(),
            P(None, "tp"),
            P(None, None, "tp"),
            P("tp"),
            P("tp"),
            P("tp"),
            P("tp"),
            P("tp", None),
        ),
        out_specs=(P("rep", None, "tp"), P("rep", None, "tp"), P("rep", "tp", None, None)),
        check_vma=False,
    )
```

profile of v0, /device:TPU:1, one launch (start us, length us, event | category | flops | bytes accessed | tf_op | source)
XLA Modules:
  0.0 319.6 jit_solution(145597851435216616)
XLA Ops:
  7.2 1.2 dynamic-slice.2
  9.7 1.2 constant_dynamic-update-slice_fusion.1
  11.0 11.9 %all-to-all-start.1 = ((bf16[32,3,2,128]{3,2,1,0:T(2,128)(2,1)}), bf16[32,3,2,128]{3,2,1,0:T(2,128)(2,1)S(1)}, u32[]{:S(2)}, u32[]{:S(2)}) async-start(bf16[32,3,2,128]{3,2,1,0:T(2,128)(2,1)} %constant_dynamic-update-slice_fusion.1), calls=%async_computation.1 | async-start | bytes 98304 | tf_op jit(solution)/shard_map/all_to_all | solution.py:151
  23.6 1.3 constant_dynamic-update-slice_fusion.2
  24.9 6.7 %all-to-all-done.1 = bf16[32,3,2,128]{3,2,1,0:T(2,128)(2,1)S(1)} async-done(((bf16[32,3,2,128]{3,2,1,0:T(2,128)(2,1)}), bf16[32,3,2,128]{3,2,1,0:T(2,128)(2,1)S(1)}, u32[]{:S(2)}, u32[]{:S(2)}) %all-to-all-start.1) | async-done | bytes 49184 | tf_op jit(solution)/shard_map/all_to_all | solution.py:151
  32.3 3.9 %all-to-all-start = ((bf16[32,3,1024]{2,1,0:T(4,128)(2,1)}), bf16[32,3,1024]{2,1,0:T(4,128)(2,1)S(1)}, u32[]{:S(2)}, u32[]{:S(2)}) async-start(bf16[32,3,1024]{2,1,0:T(4,128)(2,1)} %constant_dynamic-update-slice_fusion.2), calls=%async_computation | async-start | bytes 524288 | tf_op jit(solution)/shard_map/all_to_all | solution.py:150
  36.2 5.5 %broadcast_in_dim.235 = bf16[32,16,64,128]{3,2,1,0:T(8,128)(2,1)} broadcast(bf16[]{:T(256)} %constant.116.clone.1), dimensions={} | broadcast | bytes 8388610 | tf_op jit(solution)/shard_map/broadcast_in_dim | solution.py:145
  42.4 3.5 %all-to-all-done = bf16[32,3,1024]{2,1,0:T(4,128)(2,1)S(1)} async-done(((bf16[32,3,1024]{2,1,0:T(4,128)(2,1)}), bf16[32,3,1024]{2,1,0:T(4,128)(2,1)S(1)}, u32[]{:S(2)}, u32[]{:S(2)}) %all-to-all-start) | async-done | bytes 196640 | tf_op jit(solution)/shard_map/all_to_all | solution.py:150
  46.5 5.9 %all-to-all-start.2 = ((bf16[32,16,64,128]{3,2,1,0:T(8,128)(2,1)}), bf16[32,16,64,128]{3,2,1,0:T(8,128)(2,1)}, u32[]{:S(2)}, u32[]{:S(2)}) async-start(bf16[32,16,64,128]{3,2,1,0:T(8,128)(2,1)} %constant_dynamic-update-slice_fusion), calls=%async_computation.2 | async-start | bytes 16777216 | tf_op jit(solution)/shard_map/all_to_all | solution.py:149
  53.8 1.2 reshape.436
  55.1 1.3 reshape.439
  62.0 0.8 fusion.147
  67.2 1.3 divide_multiply_fusion.4
  68.6 0.8 convolution_bitcast_fusion.7
  69.5 1.5 copy.144
  71.0 1.5 copy.145
  72.5 4.5 %fusion.23 = f32[4,16,64,128]{3,2,1,0:T(8,128)S(1)} fusion(f32[4,32,16,64]{3,2,1,0:T(8,128)S(1)} %reshape.431, f32[4,32,16]{1,2,0:T(8,128)} %copy.147, f32[4,32,2,128]{3,1,0,2:T(8,128)S(1)} %get-tuple-element.58), kind=kOutput, calls=%fused_computation.38 | convolution fusion | flops 201457664 | bytes 3219456 | tf_op jit(solution)/shard_map/vmap(sgq,sgqp,sgn->gqpn)/dot_general | solution.py:84
  77.2 5.8 %fusion.12 = f32[4,32,1,16,64]{4,1,3,0,2:T(8,128)S(1)} fusion(f32[4,16,64,128]{3,2,1,0:T(8,128)S(1)} %fusion.23, bf16[4,16,64,128]{3,2,1,0:T(8,128)(2,1)S(1)} %copy-done, f32[4,16]{1,0:T(4,128)S(1)} %copy-done.54, f32[4,32,16]{1,2,0:T(8,128)S(1)} %copy-done.28, f32[4,32,2,128]{3,1,0,2:T(8,128)S(1)} %get-tuple-element.57), kind=kOutput, calls=%fused_computation.19 | convolution fusion | flops 203030528 | bytes 3770368 | tf_op jit(solution)/shard_map/vmap(tgn,gqpn->tgqp)/dot_general | solution.py:77
  83.0 2.1 fusion.11
  85.1 1.6 copy.151
  86.7 1.5 reshape.440
  88.8 1.5 convolution_bitcast_fusion.2
  90.3 3.0 fusion.9
  93.4 1.6 copy.136
  95.0 1.6 reshape.435
  99.6 1.2 multiply_convert_fusion.1
  100.8 1.4 gather_fusion.1
  103.0 1.5 gather_fusion
  105.4 1.1 reshape.450
  106.8 1.2 reshape.445
  107.9 2.0 convolution_bitcast_fusion.5
  110.0 125.6 %all-to-all-done.2 = bf16[32,16,64,128]{3,2,1,0:T(8,128)(2,1)} async-done(((bf16[32,16,64,128]{3,2,1,0:T(8,128)(2,1)}), bf16[32,16,64,128]{3,2,1,0:T(8,128)(2,1)}, u32[]{:S(2)}, u32[]{:S(2)}) %all-to-all-start.2) | async-done | bytes 8388640 | tf_op jit(solution)/shard_map/all_to_all | solution.py:149
  235.5 4.1 %gather_fusion.2 = bf16[3,16,64,128]{3,2,1,0:T(8,128)(2,1)S(1)} fusion(bf16[32,16,64,128]{3,2,1,0:T(8,128)(2,1)} %all-to-all-done.2, s32[1024]{0:T(1024)S(1)} %pad_clamp_fusion), kind=kCustom, calls=%fused_computation.2 | custom fusion | bytes 1572876 | tf_op jit(solution)/shard_map/jit(_take)/gather | solution.py:155
  239.7 4.5 %multiply_add_fusion = f32[3,16,64,128]{3,2,1,0:T(8,128)S(1)} fusion(f32[3,16]{1,0:T(4,128)S(1)} %fusion.141, f32[3,32,16,64]{3,2,1,0:T(8,128)} %copy-done.6, f32[3,32,16]{1,2,0:T(8,128)S(1)} %copy.174, f32[3,32,2,128]{3,1,0,2:T(8,128)S(1)} %get-tuple-element.60, bf16[3,16,64,128]{3,2,1,0:T(8,128)(2,1)S(1)} %gather_fusion.2, ...), kind=kOutput, calls=%fused_computation.9 | convolution fusion | flops 153059328 | bytes 2829312 | tf_op jit(solution)/shard_map/vmap(sgq,sgqp,sgn->gqpn)/dot_general | solution.py:84
  244.2 4.4 %fusion.21 = f32[3,32,1,16,64]{4,1,3,0,2:T(8,128)S(1)} fusion(f32[3,16,64,128]{3,2,1,0:T(8,128)S(1)} %multiply_add_fusion, f32[3,32,16]{1,2,0:T(8,128)S(1)} %copy.176, f32[3,32,2,128]{3,1,0,2:T(8,128)S(1)} %get-tuple-element.59), kind=kOutput, calls=%fused_computation.30 | convolution fusion | flops 151093248 | bytes 2039808 | tf_op jit(solution)/shard_map/vmap(tgn,gqpn->tgqp)/dot_general | solution.py:77
  248.6 1.4 fusion.20
  250.1 1.4 copy.178
  251.4 1.4 reshape.451
  252.8 3.7 %fusion.18 = f32[3,32,1,16,64]{4,1,3,0,2:T(8,128)S(1)} fusion(f32[3,32,1,16,64]{4,1,3,0,2:T(8,128)} %convolution_bitcast_fusion.5, f32[3,32,1,16,64]{4,3,1,0,2:T(8,128)} %reshape.445, f32[16]{0:T(128)S(1)} %copy-done.61, f32[3,32,16]{1,2,0:T(8,128)} %copy.161, f32[3,32,2,128]{3,1,0,2:T(8,128)} %copy-done.14, bf16[3,16,64,128]{3,2,1,0:T(8,128)(2,1)S(1)} %gather_fusion.2, ...), kind=kOutput, calls=%fused_computation.27 | convolution fusion | flops 152174592 | bytes 2826310 | tf_op jit(solution)/shard_map/vmap(tgn,gqpn->tgqp)/dot_general | solution.py:77
  256.6 1.3 copy.163
  257.9 1.4 reshape.446
  260.4 9.0 %convolution_convert_fusion = bf16[448,4096]{1,0:T(8,128)(2,1)} fusion(bf16[448,1024]{1,0:T(8,128)(2,1)S(1)} %bitcast.196, bf16[1024,4096]{1,0:T(8,128)(2,1)} %param.45), kind=kOutput, calls=%fused_computation.3 | convolution fusion | flops 3759931392 | bytes 12976128 | tf_op jit(solution)/shard_map/dot_general | solution.py:163
  270.4 3.9 %fusion.15 = bf16[3,16,64,128]{3,2,1,0:T(8,128)(2,1)} fusion(f32[3,16,64,128]{3,2,1,0:T(8,128)S(1)} %multiply_add_fusion, f32[3,16]{1,0:T(4,128)S(1)} %fusion.142, pred[3]{0:T(512)(128)(4,1)S(1)} %copy-done.39, f32[3,32,16,64]{3,2,1,0:T(8,128)S(1)} %reshape.447, f32[3,32,16]{1,2,0:T(8,128)S(1)} %copy.179, f32[3,32,2,128]{3,1,0,2:T(8,128)S(1)} %copy-done.13), kind=kOutput, calls=%fused_computation.20 | convolution fusion | flops 152666112 | bytes 3222016 | tf_op jit(solution)/shard_map/vmap(sgq,sgqp,sgn->gqpn)/dot_general | solution.py:84
  274.3 34.7 %reduce-scatter.2.cloned.1.call-done = bf16[448,512]{1,0:T(8,128)(2,1)} async-done(((bf16[448,4096]{1,0:T(8,128)(2,1)}), bf16[448,512]{1,0:T(8,128)(2,1)}) %reduce-scatter.2.cloned.1.call-update) | async-done | bytes 458768 | tf_op jit(solution)/shard_map/reduce_scatter | solution.py:166
  309.0 0.9 slice.341
  309.9 0.8 select_convert_fusion.1
  310.7 1.0 slice.340
  311.7 0.8 select_convert_fusion
  (218 shorter events, 21.3 us)
Async XLA Ops:
  11.0 20.7 %all-to-all-start.1 = ((bf16[32,3,2,128]{3,2,1,0:T(2,128)(2,1)}), bf16[32,3,2,128]{3,2,1,0:T(2,128)(2,1)S(1)}, u32[]{:S(2)}, u32[]{:S(2)}) async-start(bf16[32,3,2,128]{3,2,1,0:T(2,128)(2,1)} %constant_dynamic-update-slice_fusion.1), calls=%async_computation.1 | async-start | bytes 98304 | tf_op jit(solution)/shard_map/all_to_all | solution.py:151
  32.3 13.6 %all-to-all-start = ((bf16[32,3,1024]{2,1,0:T(4,128)(2,1)}), bf16[32,3,1024]{2,1,0:T(4,128)(2,1)S(1)}, u32[]{:S(2)}, u32[]{:S(2)}) async-start(bf16[32,3,1024]{2,1,0:T(4,128)(2,1)} %constant_dynamic-update-slice_fusion.2), calls=%async_computation | async-start | bytes 524288 | tf_op jit(solution)/shard_map/all_to_all | solution.py:150
  36.1 5.5 %copy-start.19 = (bf16[1,16,64,128]{3,2,1,0:T(8,128)(2,1)S(1)}, bf16[1,16,64,128]{3,2,1,0:T(8,128)(2,1)}, u32[]{:S(2)}) copy-start(bf16[1,16,64,128]{3,2,1,0:T(8,128)(2,1)} %param.31) | copy-start | bytes 786436
  42.3 10.7 %copy-start.36 = (bf16[4,3,1024]{2,0,1:T(4,128)(2,1)S(1)}, bf16[4,3,1024]{2,0,1:T(4,128)(2,1)}, u32[]{:S(2)}) copy-start(bf16[4,3,1024]{2,0,1:T(4,128)(2,1)} %param.24) | copy-start | bytes 73732
  42.3 10.7 %copy-start.42 = (f32[4,1024]{1,0:T(4,128)S(1)}, f32[4,1024]{1,0:T(4,128)}, u32[]{:S(2)}) copy-start(f32[4,1024]{1,0:T(4,128)} %param.39) | copy-start | bytes 49156
  42.4 10.7 %copy-start.4 = (bf16[4,64,1024]{2,1,0:T(8,128)(2,1)S(1)}, bf16[4,64,1024]{2,1,0:T(8,128)(2,1)}, u32[]{:S(2)}) copy-start(bf16[4,64,1024]{2,1,0:T(8,128)(2,1)} %param.26) | copy-start | bytes 1572868
  42.4 10.7 %slice-start = ((bf16[4,64,1024]{2,1,0:T(8,128)(2,1)}), bf16[4,32,1024]{2,1,0:T(8,128)(2,1)S(1)}, s32[]{:S(2)}) async-start(bf16[4,64,1024]{2,1,0:T(8,128)(2,1)} %param.26), calls=%async_computation.5 | async-start | bytes 524288 | tf_op jit(solution)/shard_map/vmap()/slice | solution.py:41
  46.5 189.0 %all-to-all-start.2 = ((bf16[32,16,64,128]{3,2,1,0:T(8,128)(2,1)}), bf16[32,16,64,128]{3,2,1,0:T(8,128)(2,1)}, u32[]{:S(2)}, u32[]{:S(2)}) async-start(bf16[32,16,64,128]{3,2,1,0:T(8,128)(2,1)} %constant_dynamic-update-slice_fusion), calls=%async_computation.2 | async-start | bytes 16777216 | tf_op jit(solution)/shard_map/all_to_all | solution.py:149
  52.4 256.6 %reduce-scatter.2.cloned.1.call-start = ((), (), s32[]{:S(2)}) async-start(), calls=%async_computation.4 | async-start | bytes 4128768 | tf_op jit(solution)/shard_map/reduce_scatter | solution.py:166
  57.4 4.5 %copy-start.15 = (bf16[4,64,2,128]{3,2,1,0:T(2,128)(2,1)S(1)}, bf16[4,64,2,128]{3,2,1,0:T(2,128)(2,1)}, u32[]{:S(2)}) copy-start(bf16[4,64,2,128]{3,2,1,0:T(2,128)(2,1)} %param.27) | copy-start | bytes 393220
  58.3 5.1 %copy-start.62 = (bf16[4,3,2,128]{3,2,1,0:T(2,128)(2,1)S(1)}, bf16[4,3,2,128]{3,2,1,0:T(2,128)(2,1)}, u32[]{:S(2)}) copy-start(bf16[4,3,2,128]{3,2,1,0:T(2,128)(2,1)} %param.25) | copy-start | bytes 18436
  58.6 8.1 %copy-start.63 = (f32[4,2,128]{2,1,0:T(2,128)S(1)}, f32[4,2,128]{2,1,0:T(2,128)}, u32[]{:S(2)}) copy-start(f32[4,2,128]{2,1,0:T(2,128)} %param.40) | copy-start | bytes 12292
  67.2 9.8 %copy-start = (bf16[4,16,64,128]{3,2,1,0:T(8,128)(2,1)S(1)}, bf16[4,16,64,128]{3,2,1,0:T(8,128)(2,1)}, u32[]{:S(2)}) copy-start(bf16[4,16,64,128]{3,2,1,0:T(8,128)(2,1)} %param.23) | copy-start | bytes 3145732
  72.5 4.6 %copy-start.28 = (f32[4,32,16]{1,2,0:T(8,128)S(1)}, f32[4,32,16]{1,2,0:T(8,128)}, u32[]{:S(2)}) copy-start(f32[4,32,16]{1,2,0:T(8,128)} %copy.149) | copy-start | bytes 24580
  72.5 4.6 %copy-start.54 = (f32[4,16]{1,0:T(4,128)S(1)}, f32[4,16]{1,0:T(4,128)}, u32[]{:S(2)}) copy-start(f32[4,16]{1,0:T(4,128)} %exp.147) | copy-start | bytes 772
  72.5 10.4 %copy-start.33 = (pred[32,32]{1,0:T(8,128)(4,1)}, pred[32,32]{1,0:T(8,128)(4,1)S(1)}, u32[]{:S(2)}) copy-start(pred[32,32]{1,0:T(8,128)(4,1)S(1)} %iota_compare_fusion) | copy-start | bytes 3076
  77.1 5.9 %copy-start.2 = (f32[4,32,16,64]{3,2,1,0:T(8,128)S(1)}, f32[4,32,16,64]{3,2,1,0:T(8,128)}, u32[]{:S(2)}) copy-start(f32[4,32,16,64]{3,2,1,0:T(8,128)} %reshape.436) | copy-start | bytes 1572868
  77.1 5.9 %copy-start.3 = (f32[4,32,1,16,64]{4,3,1,0,2:T(8,128)S(1)}, f32[4,32,1,16,64]{4,3,1,0,2:T(8,128)}, u32[]{:S(2)}) copy-start(f32[4,32,1,16,64]{4,3,1,0,2:T(8,128)} %reshape.439) | copy-start | bytes 1572868
  77.1 5.9 %copy-start.18 = (f32[4,32,32]{2,1,0:T(8,128)S(1)}, f32[4,32,32]{2,1,0:T(8,128)}, u32[]{:S(2)}) copy-start(f32[4,32,32]{2,1,0:T(8,128)} %copy.144) | copy-start | bytes 49156
  77.1 5.9 %copy-start.29 = (f32[4,32,16]{1,2,0:T(8,128)S(1)}, f32[4,32,16]{1,2,0:T(8,128)}, u32[]{:S(2)}) copy-start(f32[4,32,16]{1,2,0:T(8,128)} %copy.145) | copy-start | bytes 24580
  77.1 5.9 %copy-start.59 = (f32[16]{0:T(128)S(1)}, f32[16]{0:T(128)}, u32[]{:S(2)}) copy-start(f32[16]{0:T(128)} %param.43) | copy-start | bytes 196
  85.1 3.5 %copy-start.21 = (f32[4,32,16]{2,1,0:T(8,128)S(1)}, f32[4,32,16]{2,1,0:T(8,128)}, u32[]{:S(2)}) copy-start(f32[4,32,16]{2,1,0:T(8,128)} %get-tuple-element.42) | copy-start | bytes 24580
  85.1 3.6 %copy-start.20 = (f32[4,32,16]{2,1,0:T(8,128)S(1)}, f32[4,32,16]{2,1,0:T(8,128)}, u32[]{:S(2)}) copy-start(f32[4,32,16]{2,1,0:T(8,128)} %get-tuple-element.35) | copy-start | bytes 24580
  85.1 3.7 %copy-start.34 = (pred[32,32]{1,0:T(8,128)(4,1)S(1)}, pred[32,32]{1,0:T(8,128)(4,1)}, u32[]{:S(2)}) copy-start(pred[32,32]{1,0:T(8,128)(4,1)} %copy-done.33) | copy-start | bytes 3076
  85.1 3.6 %copy-start.35 = (f32[4,32,16]{1,2,0:T(8,128)S(1)}, f32[4,32,16]{1,2,0:T(8,128)}, u32[]{:S(2)}) copy-start(f32[4,32,16]{1,2,0:T(8,128)} %copy.127) | copy-start | bytes 24580
  86.7 3.6 %copy-start.60 = (f32[16]{0:T(128)S(1)}, f32[16]{0:T(128)}, u32[]{:S(2)}) copy-start(f32[16]{0:T(128)} %param.43) | copy-start | bytes 196
  93.3 3.3 %copy-start.64 = (s32[32]{0:T(128)S(1)}, s32[32]{0:T(128)}, u32[]{:S(2)}) copy-start(s32[32]{0:T(128)} %param.38) | copy-start | bytes 388
  93.3 3.4 %copy-start.16 = (bf16[3,64,2,128]{3,2,1,0:T(2,128)(2,1)S(1)}, bf16[3,64,2,128]{3,2,1,0:T(2,128)(2,1)}, u32[]{:S(2)}) copy-start(bf16[3,64,2,128]{3,2,1,0:T(2,128)(2,1)} %param.35) | copy-start | bytes 294916
  93.4 3.6 %copy-start.43 = (f32[3,1,16]{2,1,0:T(1,128)S(1)}, f32[3,1,16]{2,1,0:T(1,128)}, u32[]{:S(2)}) copy-start(f32[3,1,16]{2,1,0:T(1,128)} %slice.342) | copy-start | bytes 580
  93.4 3.6 %copy-start.45 = (f32[3,1,16]{2,1,0:T(1,128)S(1)}, f32[3,1,16]{2,1,0:T(1,128)}, u32[]{:S(2)}) copy-start(f32[3,1,16]{2,1,0:T(1,128)} %slice.339) | copy-start | bytes 580
  93.4 3.6 %copy-start.23 = (bf16[3,32,16]{2,1,0:T(8,128)(2,1)S(1)}, bf16[3,32,16]{2,1,0:T(8,128)(2,1)}, u32[]{:S(2)}) copy-start(bf16[3,32,16]{2,1,0:T(8,128)(2,1)} %copy-done.22) | copy-start | bytes 9220
  93.4 3.6 %copy-start.25 = (bf16[3,32,16]{2,1,0:T(8,128)(2,1)S(1)}, bf16[3,32,16]{2,1,0:T(8,128)(2,1)}, u32[]{:S(2)}) copy-start(bf16[3,32,16]{2,1,0:T(8,128)(2,1)} %copy-done.24) | copy-start | bytes 9220
  93.4 3.6 %copy-start.56 = (f32[16]{0:T(128)S(1)}, f32[16]{0:T(128)}, u32[]{:S(2)}) copy-start(f32[16]{0:T(128)} %param.41) | copy-start | bytes 196
  95.0 4.1 %copy-start.8 = (bf16[4,64,1024]{2,1,0:T(8,128)(2,1)S(1)}, bf16[4,64,1024]{2,1,0:T(8,128)(2,1)}, u32[]{:S(2)}) copy-start(bf16[4,64,1024]{2,1,0:T(8,128)(2,1)} %param.28) | copy-start | bytes 1572868
  97.7 4.6 %copy-start.47 = (f32[2,128]{1,0:T(2,128)S(1)}, f32[2,128]{1,0:T(2,128)}, u32[]{:S(2)}) copy-start(f32[2,128]{1,0:T(2,128)} %copy-done.46) | copy-start | bytes 3076
  97.7 4.6 %copy-start.49 = (f32[2,128]{1,0:T(2,128)S(1)}, f32[2,128]{1,0:T(2,128)}, u32[]{:S(2)}) copy-start(f32[2,128]{1,0:T(2,128)} %copy-done.48) | copy-start | bytes 3076
  97.7 4.6 %copy-start.51 = (f32[2,128]{1,0:T(2,128)S(1)}, f32[2,128]{1,0:T(2,128)}, u32[]{:S(2)}) copy-start(f32[2,128]{1,0:T(2,128)} %copy-done.50) | copy-start | bytes 3076
  97.7 4.6 %copy-start.53 = (f32[2,128]{1,0:T(2,128)S(1)}, f32[2,128]{1,0:T(2,128)}, u32[]{:S(2)}) copy-start(f32[2,128]{1,0:T(2,128)} %copy-done.52) | copy-start | bytes 3076
  99.1 140.5 %copy-start.38 = (pred[3]{0:T(512)(128)(4,1)}, pred[3]{0:T(512)(128)(4,1)S(1)}, u32[]{:S(2)}) copy-start(pred[3]{0:T(512)(128)(4,1)S(1)} %fusion.139) | copy-start | bytes 13
  99.1 140.5 %copy-start.57 = (pred[3]{0:T(512)(128)(4,1)}, pred[3]{0:T(512)(128)(4,1)S(1)}, u32[]{:S(2)}) copy-start(pred[3]{0:T(512)(128)(4,1)S(1)} %compare_and_fusion) | copy-start | bytes 13
  99.1 5.5 %copy-start.7 = (bf16[3,64,1024]{2,1,0:T(8,128)(2,1)S(1)}, bf16[3,64,1024]{2,1,0:T(8,128)(2,1)}, u32[]{:S(2)}) copy-start(bf16[3,64,1024]{2,1,0:T(8,128)(2,1)} %param.34) | copy-start | bytes 1179652
  99.2 5.5 %slice-start.1 = ((bf16[3,64,1024]{2,1,0:T(8,128)(2,1)}), bf16[3,32,1024]{2,1,0:T(8,128)(2,1)S(1)}, s32[]{:S(2)}) async-start(bf16[3,64,1024]{2,1,0:T(8,128)(2,1)} %param.34), calls=%async_computation.6 | async-start | bytes 393216 | tf_op jit(solution)/shard_map/vmap()/slice | solution.py:41
  102.4 137.2 %copy-start.14 = (f32[3,32,2,128]{3,1,0,2:T(8,128)}, f32[3,32,2,128]{3,1,0,2:T(8,128)S(1)}, u32[]{:S(2)}) copy-start(f32[3,32,2,128]{3,1,0,2:T(8,128)S(1)} %get-tuple-element.60) | copy-start | bytes 294916
  102.4 141.8 %copy-start.12 = (f32[3,32,2,128]{3,1,0,2:T(8,128)}, f32[3,32,2,128]{3,1,0,2:T(8,128)S(1)}, u32[]{:S(2)}) copy-start(f32[3,32,2,128]{3,1,0,2:T(8,128)S(1)} %get-tuple-element.59) | copy-start | bytes 294916
  106.7 128.8 %copy-start.6 = (f32[3,32,16,64]{3,2,1,0:T(8,128)}, f32[3,32,16,64]{3,2,1,0:T(8,128)S(1)}, u32[]{:S(2)}) copy-start(f32[3,32,16,64]{3,2,1,0:T(8,128)S(1)} %reshape.442) | copy-start | bytes 1179652
  239.7 8.9 %copy-start.5 = (f32[3,32,1,16,64]{4,3,1,0,2:T(8,128)S(1)}, f32[3,32,1,16,64]{4,3,1,0,2:T(8,128)}, u32[]{:S(2)}) copy-start(f32[3,32,1,16,64]{4,3,1,0,2:T(8,128)} %reshape.450) | copy-start | bytes 1179652
  239.7 8.9 %copy-start.26 = (f32[3,32,16]{1,2,0:T(8,128)S(1)}, f32[3,32,16]{1,2,0:T(8,128)}, u32[]{:S(2)}) copy-start(f32[3,32,16]{1,2,0:T(8,128)} %copy.165) | copy-start | bytes 18436
  239.7 8.9 %copy-start.61 = (f32[16]{0:T(128)S(1)}, f32[16]{0:T(128)}, u32[]{:S(2)}) copy-start(f32[16]{0:T(128)} %param.43) | copy-start | bytes 196
  (24 other events, 45.8 us)
Sparse Core Ops, SparseCore 0:
  269.6 39.3 reduce-scatter.1
where the time goes:
time: 325 us; the launch traced here: 320 us
  waiting for transfers between devices  170 us (52%)
  local copies, waits for them, and re-layouts  53.1 us (16%)
  matrix products  47.3 us (15%)
  starting transfers between devices  22.2 us (7%)
  between operations  16.8 us (5%)
  other arithmetic  9.73 us (3%)
    all_to_all x1, waiting for transfers between devices, on_device(): lax.all_to_all(place_row(hand_state), 'rep', split_axis=0, concat_axis=0,...  126 us
    reduce_scatter x1, waiting for transfers between devices, on_device(): lax.psum_scatter(partial_sum.astype(jnp.bfloat16), 'tp', scatter_dimensio...  34.7 us
    dot_general x4, matrix products, decode_request(): jnp.einsum('tgn,gqpn->tgqp', coeff_c, grouped, precision=highest)  16.9 us
    dot_general x3, matrix products, decode_request(): jnp.einsum('sgq,sgqp,sgn->gqpn', tail_weight, x_conv, coeff_b, precision=...  12.9 us
    all_to_all x1, starting transfers between devices, on_device(): lax.all_to_all(place_row(hand_conv_bc), 'rep', split_axis=0, concat_axis=...  11.9 us
    dot_general x1, matrix products, on_device(): jnp.dot(joined.reshape(-1, joined.shape[-1]), out_w, preferred_element_ty...  9.04 us
    dot_general x4, matrix products, decode_request(): y_inner = jnp.einsum('tsgq,sgqp->tgqp', weights, x_conv, precision=highest)  7.01 us
    gather x3, local copies, waits for them, and re-layouts, on_device(): jnp.take(values_array, sources, axis=0)  6.98 us
  transfers between devices with their start and end apart: 4, of which 4 were waited for; matrix products, arithmetic and copies ran while one was open for 21% of the time, Pallas kernels for 0%

commit v1 on v0

v1 whole, which is shorter than its diff:
```python
import functools

import jax
import jax.numpy as jnp
from jax import lax
from jax.experimental import pallas as pl
from jax.experimental.pallas import tpu as pltpu
from jax.sharding import PartitionSpec as P

F32 = jnp.float32
BF16 = jnp.bfloat16
ROWS = 64
INNER = 1024
STATE = 128
HEADS = 16
PAIRS = HEADS // 2
TAPS = 4
CAP = 3
NX, NZ = 4, 8
NY = 4
TOP = 8
PACK = 1056
HALF = PACK // 2
EARLY = (0, 1, 7, 2, 6)
LATE = (3, 5, 4)
ORDER = EARLY + LATE
VMEM_LIMIT = 48 * 1024 * 1024


def lanes_of(shape):
    return lax.broadcasted_iota(jnp.int32, shape, 1)


def rows_of(shape):
    return lax.broadcasted_iota(jnp.int32, shape, 0)


def mix_rows(win_x, win_bc, dt_pad, gated, dt, z_ref, params, load_state, store_state, out_ref):
    wx, wbc, dt_bias, a_log, d_skip, norm_w = params
    acc = win_bc[TOP - 3 : TOP - 3 + ROWS, :] * wbc[0:1, :]
    for k in range(1, TAPS):
        acc += win_bc[TOP - 3 + k : TOP - 3 + k + ROWS, :] * wbc[k : k + 1, :]
    bcc = acc / (1.0 + jnp.exp(-acc))
    coeff_b = bcc[:, :STATE].astype(BF16)
    coeff_c = bcc[:, STATE:].astype(BF16)

    raw = dt + dt_bias[...]
    step = jnp.maximum(raw, 0.0) + jnp.log(1.0 + jnp.exp(-jnp.abs(raw)))
    dt_pad[...] = jnp.zeros_like(dt_pad)
    dt_pad[0, :, 0:HEADS] = step
    dt_pad[1, :, 0:HEADS] = step * -jnp.exp(a_log[...])
    size = dt_pad[0]
    cum = dt_pad[1]
    row = rows_of((ROWS, 128))
    for shift in (1, 2, 4, 8, 16, 32):
        cum = cum + jnp.where(row >= shift, pltpu.roll(cum, shift, 0), 0.0)

    lane = lanes_of((ROWS, 128))
    left = lane < 64
    source = jnp.where(left, lane, lane - 64)
    causal = row >= source
    diagonal = row == source
    twice_b = jnp.concatenate([coeff_b, coeff_b], axis=0)
    scores = lax.dot_general(
        coeff_c, twice_b, (((1,), (1,)), ((), ())), preferred_element_type=F32
    )
    squares = jnp.zeros((ROWS, 128), F32)
    for pair in range(PAIRS):
        cols = slice(pair * 128, pair * 128 + 128)
        first, second = 2 * pair, 2 * pair + 1

        def spread(values):
            return jnp.where(left, values[:, first : first + 1], values[:, second : second + 1])

        acc = win_x[TOP - 3 : TOP - 3 + ROWS, cols] * wx[0:1, cols]
        for k in range(1, TAPS):
            acc += win_x[TOP - 3 + k : TOP - 3 + k + ROWS, cols] * wx[k : k + 1, cols]
        x_conv = acc / (1.0 + jnp.exp(-acc))
        cum_here = spread(cum)
        x_size = x_conv * spread(size)
        cum_source = jnp.sum(jnp.where(diagonal, cum_here, 0.0), axis=0, keepdims=True)
        decay = jnp.where(causal, jnp.exp(jnp.where(causal, cum_here - cum_source, 0.0)), 0.0)
        weights = (decay * scores).astype(BF16)
        blocks = jnp.concatenate(
            [jnp.where(left, x_size, 0.0), jnp.where(left, 0.0, x_size)], axis=0
        ).astype(BF16)
        y = jnp.dot(weights, blocks, preferred_element_type=F32)
        held = load_state(pair)
        y += jnp.exp(cum_here) * lax.dot_general(
            coeff_c, held, (((1,), (1,)), ((), ())), preferred_element_type=F32
        )
        y += spread(d_skip[...]) * x_conv
        if store_state is not None:
            last = cum_here[ROWS - 1 : ROWS, :]
            tail = (jnp.exp(last - cum_here) * x_size).astype(BF16)
            update = lax.dot_general(
                tail, coeff_b, (((0,), (0,)), ((), ())), preferred_element_type=F32
            )
            final = jnp.exp(cum[ROWS - 1 : ROWS, :])
            keep = jnp.where(
                rows_of((128, 128)) < 64, final[:, first : first + 1], final[:, second : second + 1]
            )
            store_state(pair, held.astype(F32) * keep + update)
        gate = z_ref[0, :, cols].astype(F32)
        g = y * (gate / (1.0 + jnp.exp(-gate)))
        gated[:, cols] = g
        squares += g * g
    scale = lax.rsqrt(jnp.sum(squares, axis=1, keepdims=True) * (1.0 / INNER) + 1e-05)
    out_ref[0] = (gated[...] * scale * norm_w[...]).astype(BF16)


def resident_kernel(
    count, state, conv_x, conv_bc, x, bc, z, dt,
    wx, wbc, dt_bias, a_log, d_skip, norm_w, out, win_x, win_bc, dt_pad, gated,
):
    slot = pl.program_id(0)

    @pl.when(slot < count[0])
    def _():
        win_x[TOP - 3 : TOP, :] = conv_x[0].astype(F32)
        win_x[TOP:, :] = x[0].astype(F32)
        win_bc[TOP - 3 : TOP, :] = conv_bc[0].astype(F32)
        win_bc[TOP:, :] = bc[0].astype(F32)

        def load_state(pair):
            return state[0, 2 * pair : 2 * pair + 2].reshape(128, STATE)

        mix_rows(
            win_x, win_bc, dt_pad, gated, dt[0].astype(F32), z,
            (wx, wbc, dt_bias, a_log, d_skip, norm_w), load_state, None, out,
        )

    @pl.when(slot >= count[0])
    def _():
        out[...] = jnp.zeros_like(out)


ROW_SCRATCH = [
    pltpu.VMEM((TOP + ROWS, INNER), F32),
    pltpu.VMEM((TOP + ROWS, 2 * STATE), F32),
    pltpu.VMEM((2, ROWS, 128), F32),
    pltpu.VMEM((ROWS, INNER), F32),
]


def whole(array):
    return pl.BlockSpec(array.shape, lambda *_: (0,) * array.ndim)


def per_slot(shape):
    return pl.BlockSpec((1,) + shape, lambda i, *_: (i,) + (0,) * len(shape))


def resident_rows(count, state, conv_x, conv_bc, x, bc, z, dt, params):
    slots = state.shape[0]
    return pl.pallas_call(
        resident_kernel,
        grid_spec=pltpu.PrefetchScalarGridSpec(
            num_scalar_prefetch=1,
            grid=(slots,),
            in_specs=[per_slot(a.shape[1:]) for a in (state, conv_x, conv_bc, x, bc, z, dt)]
            + [whole(a) for a in params],
            out_specs=per_slot((ROWS, INNER)),
            scratch_shapes=ROW_SCRATCH,
        ),
        out_shape=jax.ShapeDtypeStruct((slots, ROWS, INNER), BF16),
        compiler_params=pltpu.CompilerParams(vmem_limit_bytes=VMEM_LIMIT),
        cost_estimate=pl.CostEstimate(flops=400_000_000, bytes_accessed=16_000_000, transcendentals=0),
        name="resident_rows",
    )(count, state, conv_x, conv_bc, x, bc, z, dt, *params)


def line_hits(assign, target, column):
    target_z = lax.rem(target, NZ)
    return [
        (assign[column * NZ + lax.rem(target_z + NZ - offset, NZ)] == target).astype(jnp.int32)
        for offset in ORDER
    ]


def round_ranks(hits):
    early = functools.reduce(jnp.maximum, hits[: len(EARLY)])
    ranks, seen = [], jnp.int32(0)
    for hit in hits:
        ranks.append(seen + (1 - early))
        seen = seen + hit
    return ranks


def packet_copies(packets, offset, dst, sem):
    if offset == 4:
        low, high = packets[4]
        return [
            pltpu.make_async_copy(low, dst.at[pl.ds(0, HALF)], sem),
            pltpu.make_async_copy(high, dst.at[pl.ds(HALF, HALF)], sem),
        ]
    return [pltpu.make_async_copy(packets[offset], dst, sem)]


def forward_kernel(rounds, offsets, info, *refs):
    count = len(offsets) + (1 if 4 in offsets else 0)
    ins, outs, sems = refs[:count], refs[count:-1], refs[-1]
    packets, at = {}, 0
    for offset in offsets:
        if offset == 4:
            packets[4] = (ins[at], ins[at + 1])
            at += 2
        else:
            packets[offset] = ins[at]
            at += 1
    me = info[32]
    column, z = lax.div(me, NZ), lax.rem(me, NZ)
    todo = []
    for shift in range(1, NX):
        target = lax.rem(column + shift, NX) * NZ + z
        hits = line_hits(info, target, column)
        ranks = round_ranks(hits)
        for n, wanted in enumerate(rounds):
            slot = n * (NX - 1) + shift - 1
            for offset, hit, rank in zip(ORDER, hits, ranks):
                if offset in packets:
                    todo.append(
                        ((hit == 1) & (rank == wanted),
                         packet_copies(packets, offset, outs[slot], sems.at[slot]))
                    )
    for wanted, copies in todo:
        @pl.when(wanted)
        def _(copies=copies):
            for copy in copies:
                copy.start()
    for wanted, copies in todo:
        @pl.when(wanted)
        def _(copies=copies):
            for copy in copies:
                copy.wait()


def forward(rounds, offsets, info, packets):
    count = len(rounds) * (NX - 1)
    return pl.pallas_call(
        functools.partial(forward_kernel, rounds, offsets),
        in_specs=[pl.BlockSpec(memory_space=pltpu.SMEM)]
        + [pl.BlockSpec(memory_space=pl.ANY)] * len(packets),
        out_specs=[pl.BlockSpec(memory_space=pl.ANY)] * count,
        out_shape=[jax.ShapeDtypeStruct((PACK, 128), BF16)] * count,
        scratch_shapes=[pltpu.SemaphoreType.DMA((count,))],
        cost_estimate=pl.CostEstimate(flops=0, bytes_accessed=3_000_000, transcendentals=0),
        name="forward",
    )(info, *packets)


def blank_kernel(info, *outs):
    pass


def blank(info, count):
    return pl.pallas_call(
        blank_kernel,
        in_specs=[pl.BlockSpec(memory_space=pltpu.SMEM)],
        out_specs=[pl.BlockSpec(memory_space=pl.ANY)] * count,
        out_shape=[jax.ShapeDtypeStruct((PACK, 128), BF16)] * count,
        name="blank",
    )(info)


PACKETS = 9
ARRIVED = 4 * (NX - 1)


def slot_kernel(info, *refs):
    line, rest = refs[:PACKETS], refs[PACKETS:]
    came, rest = rest[:ARRIVED], rest[ARRIVED:]
    (x, bc, z, dt, wx, wbc, dt_bias, a_log, d_skip, norm_w, out, state,
     held, valid, win_x, win_bc, dt_pad, gated, sems) = rest
    packets = {o: line[i] for i, o in enumerate(ORDER[:-1])}
    packets[4] = (line[PACKETS - 2], line[PACKETS - 1])
    slot = pl.program_id(0)
    me = info[32]
    column, my_z = lax.div(me, NZ), lax.rem(me, NZ)

    @pl.when(slot == 0)
    def _():
        before = jnp.int32(0)
        order = []
        for request in range(NX * NZ):
            mine = (info[request] == me).astype(jnp.int32)
            order.append(before)
            before = before + mine
        valid[0] = before
        for shift in range(NX):
            sender = lax.rem(column + NX - shift, NX)
            hits = line_hits(info, me, sender)
            ranks = round_ranks(hits)
            for offset, hit, rank in zip(ORDER, hits, ranks):
                source = sender * NZ + lax.rem(my_z + NZ - offset, NZ)
                place = jnp.int32(0)
                for request in range(NX * NZ):
                    place = jnp.where(source == request, order[request], place)

                @pl.when(hit == 1)
                def _(shift=shift, offset=offset, rank=rank, place=place):
                    if shift == 0:
                        for copy in packet_copies(packets, offset, held.at[place], sems.at[place]):
                            copy.start()
                    else:
                        for n in range(4):
                            @pl.when(rank == n)
                            def _(n=n):
                                pltpu.make_async_copy(
                                    came[n * (NX - 1) + shift - 1], held.at[place], sems.at[place]
                                ).start()

    live = slot < valid[0]

    @pl.when(live)
    def _():
        win_x[TOP:, :] = x[0].astype(F32)
        win_bc[TOP:, :] = bc[0].astype(F32)
        pltpu.make_async_copy(held.at[slot], held.at[slot], sems.at[slot]).wait()
        conv = held[slot, 1024:PACK, :].astype(F32)
        for k in range(TAPS - 1):
            for b in range(8):
                win_x[TOP - 3 + k : TOP - 2 + k, 128 * b : 128 * b + 128] = conv[
                    8 * k + b : 8 * k + b + 1
                ]
            for b in range(2):
                win_bc[TOP - 3 + k : TOP - 2 + k, 128 * b : 128 * b + 128] = conv[
                    24 + 2 * k + b : 25 + 2 * k + b
                ]

        def load_state(pair):
            return held[slot, 128 * pair : 128 * pair + 128, :]

        def store_state(pair, value):
            state[0, 2 * pair : 2 * pair + 2] = value.astype(BF16).reshape(2, 64, STATE)

        mix_rows(
            win_x, win_bc, dt_pad, gated, dt[0].astype(F32), z,
            (wx, wbc, dt_bias, a_log, d_skip, norm_w), load_state, store_state, out,
        )

    @pl.when(jnp.logical_not(live))
    def _():
        out[...] = jnp.zeros_like(out)
        state[...] = jnp.zeros_like(state)


def slot_rows(info, line, came, x, bc, z, dt, params):
    slots = x.shape[0]
    return pl.pallas_call(
        slot_kernel,
        grid=(slots,),
        in_specs=[pl.BlockSpec(memory_space=pltpu.SMEM)]
        + [pl.BlockSpec(memory_space=pl.ANY)] * (PACKETS + ARRIVED)
        + [per_slot(a.shape[1:]) for a in (x, bc, z, dt)]
        + [whole(a) for a in params],
        out_specs=[per_slot((ROWS, INNER)), per_slot((HEADS, 64, STATE))],
        out_shape=[
            jax.ShapeDtypeStruct((slots, ROWS, INNER), BF16),
            jax.ShapeDtypeStruct((slots, HEADS, 64, STATE), BF16),
        ],
        scratch_shapes=[pltpu.VMEM((CAP, PACK, 128), BF16), pltpu.SMEM((1,), jnp.int32)]
        + ROW_SCRATCH
        + [pltpu.SemaphoreType.DMA((CAP,))],
        compiler_params=pltpu.CompilerParams(vmem_limit_bytes=VMEM_LIMIT),
        cost_estimate=pl.CostEstimate(flops=400_000_000, bytes_accessed=20_000_000, transcendentals=0),
        name="slot_rows",
    )(info, *line, *came, x, bc, z, dt, *params)


def project_kernel(blocks, rows, weight, out):
    out[0] = jnp.dot(rows[...], weight[...], preferred_element_type=F32).astype(BF16)


def project(blocks, rows, weight):
    count, width = blocks.shape[0], weight.shape[1] // 8
    return pl.pallas_call(
        project_kernel,
        grid_spec=pltpu.PrefetchScalarGridSpec(
            num_scalar_prefetch=1,
            grid=(count,),
            in_specs=[
                pl.BlockSpec(rows.shape, lambda i, blocks: (0, 0)),
                pl.BlockSpec((weight.shape[0], width), lambda i, blocks: (0, blocks[i])),
            ],
            out_specs=pl.BlockSpec((1, rows.shape[0], width), lambda i, blocks: (i, 0, 0)),
        ),
        out_shape=jax.ShapeDtypeStruct((count, rows.shape[0], width), BF16),
        compiler_params=pltpu.CompilerParams(vmem_limit_bytes=VMEM_LIMIT),
        cost_estimate=pl.CostEstimate(
            flops=2 * count * rows.shape[0] * weight.shape[0] * width,
            bytes_accessed=6_000_000, transcendentals=0,
        ),
        name="project",
    )(blocks, rows, weight)


def reduce_out(normed, out_w, sent, kept):
    slots = normed.shape[0]
    rows = normed.reshape(slots * ROWS, INNER)
    mates = [(t, t ^ 1) for t in range(2 * NY)]
    from_mate = lax.ppermute(project(sent, rows, out_w), "tp", mates)
    own = project(kept, rows, out_w)
    chip = [own[k].astype(F32) + from_mate[k].astype(F32) for k in range(NY)]
    total = chip[0]
    for k in range(1, NY):
        shifted = [(t, (t + 2 * k) % (2 * NY)) for t in range(2 * NY)]
        total = total + lax.ppermute(chip[k].astype(BF16), "tp", shifted).astype(F32)
    return total.astype(BF16).reshape(slots, ROWS, -1)


def along_z(array, step):
    pairs = [(x * NZ + z, x * NZ + (z + step) % NZ) for x in range(NX) for z in range(NZ)]
    return lax.ppermute(array, "rep", pairs)


def along_x(arrays):
    return [
        lax.ppermute(
            array, "rep",
            [(x * NZ + z, (x + shift) % NX * NZ + z) for x in range(NX) for z in range(NZ)],
        )
        for shift, array in zip([1, 2, 3] * 4, arrays)
    ]


def on_device(
    res_state, res_conv_x, res_conv_bc, res_x, res_bc, res_z, res_dt, res_count,
    hand_state, hand_conv_x, hand_conv_bc, slot_x, slot_bc, slot_z, slot_dt,
    assignment, conv_wx, conv_wbc, dt_bias, a_log, d_skip, norm_w, out_w,
):
    me = lax.axis_index("rep")
    tp = lax.axis_index("tp")
    info = jnp.concatenate([assignment, me[None].astype(jnp.int32)])
    packet = jnp.concatenate(
        [
            hand_state.reshape(-1, STATE),
            hand_conv_x.reshape(-1, STATE),
            hand_conv_bc.reshape(-1, STATE),
            jnp.zeros((2, STATE), BF16),
        ],
        axis=0,
    )
    up1, down1 = along_z(packet, 1), along_z(packet, -1)
    up2, down2 = along_z(packet, 2), along_z(packet, -2)

    params = (
        conv_wx, conv_wbc.reshape(TAPS, 2 * STATE), dt_bias[None], a_log[None], d_skip[None],
        norm_w[None],
    )
    res_normed = resident_rows(
        res_count, res_state, res_conv_x, res_conv_bc.reshape(-1, TAPS - 1, 2 * STATE), res_x,
        res_bc.reshape(-1, ROWS, 2 * STATE), res_z, res_dt, params,
    )
    chip, core = tp // 2, tp % 2
    turns = (chip + jnp.arange(NY, dtype=jnp.int32)) % NY
    sent, kept = 2 * turns + 1 - core, 2 * turns + core

    early = [packet, up1, down1, up2, down2]
    first = along_x(forward((0,), EARLY, info, early))
    up3, down3 = along_z(up2, 1), along_z(down2, -1)
    up4, down4 = along_z(up2[:HALF], 2), along_z(down2[HALF:], -2)
    line = early + [up3, down3, up4, down4]
    res_out = reduce_out(res_normed, out_w, sent, kept)
    second = along_x(forward((1,), ORDER, info, line))

    ids = jnp.arange(NX * NZ)
    goes = assignment[None, :] == ids[:, None]
    offset = (ids[:, None] - ids[None, :]) % NZ
    far = (offset > 2) & (offset < 6)
    all_hits = jnp.sum(goes.reshape(-1, NX, NZ), axis=2)
    near_hits = jnp.sum((goes & ~far).reshape(-1, NX, NZ), axis=2)
    across = (ids[:, None] // NZ) != jnp.arange(NX)[None, :]
    more = jnp.any(across & (all_hits - jnp.minimum(near_hits, 1) > 1))
    third = lax.cond(
        more,
        lambda *held: tuple(along_x(forward((2, 3), ORDER, held[0], held[1:]))),
        lambda *held: tuple(blank(held[0], 2 * (NX - 1))),
        info, *line,
    )
    slot_normed, slot_state = slot_rows(
        info, line, first + second + list(third), slot_x,
        slot_bc.reshape(-1, ROWS, 2 * STATE), slot_z, slot_dt, params,
    )
    slot_out = reduce_out(slot_normed, out_w, sent, kept)
    return res_out, slot_out, slot_state


def solution(mesh):
    rows = P("rep", None, "tp")
    pairs = P("rep", None, None, "tp")
    states = P("rep", "tp", None, None)
    return jax.shard_map(
        on_device,
        mesh=mesh,
        in_specs=(
            states, rows, pairs, rows, pairs, rows, rows, P("rep"),
            states, rows, pairs, rows, pairs, rows, rows,
            P(), P(None, "tp"), P(None, None, "tp"), P("tp"), P("tp"), P("tp"), P("tp"),
            P("tp", None),
        ),
        out_specs=(rows, rows, states),
        check_vma=False,
    )
```

time: 325 us -> 146 us (0.45); the launches traced: 320 us -> 144 us
  waiting for transfers between devices: 170 us -> 25.2 us
  matrix products: 47.3 us -> 0 us
  Pallas kernels: 0 us -> 36.3 us
  local copies, waits for them, and re-layouts: 53.1 us -> 22.8 us
  starting transfers between devices: 22.2 us -> 51.6 us
  between operations: 16.8 us -> 2.26 us
  other arithmetic: 9.73 us -> 5.63 us
    all_to_all x3 -> x0, waiting for transfers between devices: 136 us -> none  [the longest x1 126 us: on_device(): lax.all_to_all(place_row(hand_state), 'rep', split_axis=0, concat_axis=0,...]
    ppermute x0 -> x22, starting transfers between devices: none -> 51.6 us  [the longest x6 18.9 us: along_x(): lax.ppermute(array, 'rep', [(x * NZ + z, (x + shift) % NX * NZ + z) for x...]
    dot_general x16 -> x0, matrix products: 47.3 us -> none  [the longest x4 16.9 us: decode_request(): jnp.einsum('tgn,gqpn->tgqp', coeff_c, grouped, precision=highest)]
    pallas_call x0 -> x9, Pallas kernels: none -> 36.3 us  [the longest x4 17.3 us: project(): pl.pallas_call(project_kernel, grid_spec=pltpu.PrefetchScalarGridSpec(num...]
    reduce_scatter x1 -> x0, waiting for transfers between devices: 34.7 us -> none  [on_device(): lax.psum_scatter(partial_sum.astype(jnp.bfloat16), 'tp', scatter_dimensio...]
    ppermute x0 -> x22, waiting for transfers between devices: none -> 25.2 us  [the longest x6 10.2 us: reduce_out(): lax.ppermute(chip[k].astype(BF16), 'tp', shifted).astype(F32)]
    all_to_all x3 -> x0, starting transfers between devices: 21.6 us -> none  [the longest x1 11.9 us: on_device(): lax.all_to_all(place_row(hand_conv_bc), 'rep', split_axis=0, concat_axis=...]
    unnamed x141 -> x49, local copies, waits for them, and re-layouts: 4.23 us -> 15.8 us
  transfers between devices with their start and end apart: 4 -> 22, of which waited for: 4 -> 7; matrix products, arithmetic and copies ran while one was open for 21% -> 10% of each run, Pallas kernels for 0% -> 25%
where the time goes in v1:
time: 146 us; the launch traced here: 144 us
  starting transfers between devices  51.6 us (35%)
  Pallas kernels  36.3 us (25%)
  waiting for transfers between devices  25.2 us (17%)
  local copies, waits for them, and re-layouts  22.8 us (16%)
  other arithmetic  5.63 us (4%)
  between operations  2.26 us (2%)
    ppermute x6, starting transfers between devices, along_x(): lax.ppermute(array, 'rep', [(x * NZ + z, (x + shift) % NX * NZ + z) for x...  18.9 us
    ppermute x8, starting transfers between devices, along_z(): return lax.ppermute(array, 'rep', pairs)  18.6 us
    pallas_call x4, Pallas kernels, project(): pl.pallas_call(project_kernel, grid_spec=pltpu.PrefetchScalarGridSpec(num...  17.3 us
    unnamed x49, local copies, waits for them, and re-layouts  15.8 us
    pallas_call x2, Pallas kernels, forward(): pl.pallas_call(functools.partial(forward_kernel, rounds, offsets), in_spe...  10.7 us
    ppermute x6, waiting for transfers between devices, reduce_out(): lax.ppermute(chip[k].astype(BF16), 'tp', shifted).astype(F32)  10.2 us
    ppermute x6, waiting for transfers between devices, along_x(): lax.ppermute(array, 'rep', [(x * NZ + z, (x + shift) % NX * NZ + z) for x...  10.2 us
    ppermute x6, starting transfers between devices, reduce_out(): lax.ppermute(chip[k].astype(BF16), 'tp', shifted).astype(F32)  8.02 us
  transfers between devices with their start and end apart: 22, of which 7 were waited for; matrix products, arithmetic and copies ran while one was open for 10% of the time, Pallas kernels for 25%

profile of v1, /device:TPU:1, one launch (start us, length us, event | category | flops | bytes accessed | tf_op | source)
XLA Modules:
  0.0 144.0 jit_solution(5393332957248034712)
XLA Ops:
  2.0 1.0 concatenate.10.refs_0_
  3.1 3.9 %collective-permute-start.12 = (bf16[1056,128]{1,0:T(8,128)(2,1)S(1)}, bf16[1056,128]{1,0:T(8,128)(2,1)}, u32[]{:S(2)}, u32[]{:S(2)}) collective-permute-start(bf16[1056,128]{1,0:T(8,128)(2,1)S(1)} %concatenate.10.refs_0_), channel_id=1, source_target_pairs={{0,16},{8,24},{16,32},{24,40},{32,48},{40,56},{48,0},{56,8},{64,80... | collective-permute-start | bytes 811016 | tf_op jit(solution)/shard_map/ppermute | solution.py:414
  7.0 3.1 %collective-permute-start.13 = (bf16[1056,128]{1,0:T(8,128)(2,1)S(1)}, bf16[1056,128]{1,0:T(8,128)(2,1)}, u32[]{:S(2)}, u32[]{:S(2)}) collective-permute-start(bf16[1056,128]{1,0:T(8,128)(2,1)S(1)} %concatenate.10.refs_0_), channel_id=1, source_target_pairs={{0,48},{8,56},{16,0},{24,8},{32,16},{40,24},{48,32},{56,40},{64,11... | collective-permute-start | bytes 811016 | tf_op jit(solution)/shard_map/ppermute | solution.py:414
  10.1 0.7 collective-permute-start.10
  10.8 1.9 %collective-permute-start.11 = (bf16[1056,128]{1,0:T(8,128)(2,1)S(1)}, bf16[1056,128]{1,0:T(8,128)(2,1)}, u32[]{:S(2)}, u32[]{:S(2)}) collective-permute-start(bf16[1056,128]{1,0:T(8,128)(2,1)S(1)} %concatenate.10.refs_0_), channel_id=1, source_target_pairs={{0,56},{8,0},{16,8},{24,16},{32,24},{40,32},{48,40},{56,48},{64,12... | collective-permute-start | bytes 811016 | tf_op jit(solution)/shard_map/ppermute | solution.py:414
  12.8 0.7 eq.25
  13.6 4.2 %collective-permute-done.12.refs_3_ = bf16[1056,128]{1,0:T(8,128)(2,1)} collective-permute-done((bf16[1056,128]{1,0:T(8,128)(2,1)S(1)}, bf16[1056,128]{1,0:T(8,128)(2,1)}, u32[]{:S(2)}, u32[]{:S(2)}) %collective-permute-start.12) | collective-permute-done | bytes 270368 | tf_op jit(solution)/shard_map/ppermute | solution.py:414
  17.9 5.2 %collective-permute-start.14 = (bf16[1056,128]{1,0:T(8,128)(2,1)}, bf16[1056,128]{1,0:T(8,128)(2,1)}, u32[]{:S(2)}, u32[]{:S(2)}) collective-permute-start(bf16[1056,128]{1,0:T(8,128)(2,1)} %collective-permute-done.12.refs_3_), channel_id=1, source_target_pairs={{0,8},{8,16},{16,24},{24,32},{32,40},{40,48},{48,56},{56,0},{64,72... | collective-permute-start | bytes 811016 | tf_op jit(solution)/shard_map/ppermute | solution.py:414
  25.5 1.0 reshape.137.bc
  26.5 0.8 copy.37.dt
  27.4 0.8 copy.35.conv_x
  29.5 0.7 pad_add_fusion.info
  30.2 0.9 slice.80
  31.1 2.6 %collective-permute-start.16 = (bf16[528,128]{1,0:T(8,128)(2,1)S(1)}, bf16[528,128]{1,0:T(8,128)(2,1)}, u32[]{:S(2)}, u32[]{:S(2)}) collective-permute-start(bf16[528,128]{1,0:T(8,128)(2,1)S(1)} %slice.80), channel_id=1, source_target_pairs={{0,16},{8,24},{16,32},{24,40},{32,48},{40,56},{48,0},{56,8},{64,80... | collective-permute-start | bytes 405512 | tf_op jit(solution)/shard_map/ppermute | solution.py:414
  33.8 0.9 slice.81
  34.7 1.1 collective-permute-start.17
  35.8 1.2 copy-done
  37.0 1.0 copy-done.1
  38.1 1.0 copy-done.2
  42.5 1.8 %resident_rows.1 = bf16[4,64,1024]{2,1,0:T(8,128)(2,1)S(1)} custom-call(s32[1]{0:T(128)S(6)} %copy.56.count, bf16[4,16,64,128]{3,2,1,0:T(8,128)(2,1)S(1)} %copy-done, bf16[4,3,1024]{2,1,0:T(4,128)(2,1)S(1)} %copy.35.conv_x, bf16[4,3,256]{2,1,0:T(4,128)(2,1)S(1)} %copy.36.conv_bc, bf16[4,64,1024]{2,1,0:T(8,128)(2,1)S(1)} %copy-done.1, ...), custom_call_target="tpu_custom_call" | custom-call | flops 400000000 | bytes 16000000 | tf_op jit(solution)/shard_map/resident_rows/pallas_call | solution.py:156
  45.2 0.7 conditional.1
  45.9 1.3 collective-permute-start.18
  47.2 12.5 %collective-permute-start.19 = (bf16[1056,128]{1,0:T(8,128)(2,1)}, bf16[1056,128]{1,0:T(8,128)(2,1)S(1)}, u32[]{:S(2)}, u32[]{:S(2)}) collective-permute-start(bf16[1056,128]{1,0:T(8,128)(2,1)} %get-tuple-element.55), channel_id=1, source_target_pairs={{0,128},{8,136},{16,144},{24,152},{32,160},{40,168},{48,176},{56,1... | collective-permute-start | bytes 811016 | tf_op jit(solution)/shard_map/ppermute | solution.py:419
  59.7 4.4 %project.5 = bf16[4,256,512]{2,1,0:T(8,128)(2,1)S(1)} custom-call(s32[4]{0:T(128)S(1)} %add_subtract_fusion.blocks, bf16[256,1024]{1,0:T(8,128)(2,1)S(1)} %bitcast.45, bf16[1024,4096]{1,0:T(8,128)(2,1)} %weight.7), custom_call_target="tpu_custom_call" | custom-call | flops 1073741824 | bytes 6000000 | tf_op jit(solution)/shard_map/project/pallas_call | solution.py:377
  64.2 4.5 %collective-permute-start.6 = (bf16[4,256,512]{2,1,0:T(8,128)(2,1)S(1)}, bf16[4,256,512]{2,1,0:T(8,128)(2,1)}, u32[]{:S(2)}, u32[]{:S(2)}) collective-permute-start(bf16[4,256,512]{2,1,0:T(8,128)(2,1)S(1)} %project.5), channel_id=1, source_target_pairs={{0,1},{1,0},{2,3},{3,2},{4,5},{5,4},{6,7},{7,6},{8,9},{9,8},{10,11... | collective-permute-start | bytes 3145736 | tf_op jit(solution)/shard_map/ppermute | solution.py:402
  68.7 2.3 %collective-permute-start.20 = (bf16[1056,128]{1,0:T(8,128)(2,1)}, bf16[1056,128]{1,0:T(8,128)(2,1)S(1)}, u32[]{:S(2)}, u32[]{:S(2)}) collective-permute-start(bf16[1056,128]{1,0:T(8,128)(2,1)} %get-tuple-element.56), channel_id=1, source_target_pairs={{0,192},{8,200},{16,208},{24,216},{32,224},{40,232},{48,240},{56,2... | collective-permute-start | bytes 811016 | tf_op jit(solution)/shard_map/ppermute | solution.py:419
  70.9 10.0 %forward.5 = (bf16[1056,128]{1,0:T(8,128)(2,1)}, bf16[1056,128]{1,0:T(8,128)(2,1)}, bf16[1056,128]{1,0:T(8,128)(2,1)}) custom-call(s32[33]{0:T(128)S(1)} %pad_add_fusion.info, bf16[1056,128]{1,0:T(8,128)(2,1)S(1)} %concatenate.10.refs_0_, bf16[1056,128]{1,0:T(8,128)(2,1)} %collective-permute-done.10.refs_1_, ...), custom_call_target="tpu_custom_call" | custom-call | bytes 3000000 | tf_op jit(solution)/shard_map/forward/pallas_call | solution.py:240
  81.1 2.6 %collective-permute-start.23 = (bf16[1056,128]{1,0:T(8,128)(2,1)}, bf16[1056,128]{1,0:T(8,128)(2,1)}, u32[]{:S(2)}, u32[]{:S(2)}) collective-permute-start(bf16[1056,128]{1,0:T(8,128)(2,1)} %get-tuple-element.59), channel_id=1, source_target_pairs={{0,192},{8,200},{16,208},{24,216},{32,224},{40,232},{48,240},{56,2... | collective-permute-start | bytes 811016 | tf_op jit(solution)/shard_map/ppermute | solution.py:419
  83.8 1.0 reshape.144.refs_22_
  84.7 1.4 copy.38.refs_24_
  86.1 9.8 %collective-permute-done.21.refs_12_ = bf16[1056,128]{1,0:T(8,128)(2,1)S(1)} collective-permute-done((bf16[1056,128]{1,0:T(8,128)(2,1)}, bf16[1056,128]{1,0:T(8,128)(2,1)S(1)}, u32[]{:S(2)}, u32[]{:S(2)}) %collective-permute-start.21) | collective-permute-done | bytes 270368 | tf_op jit(solution)/shard_map/ppermute | solution.py:419
  96.4 0.8 copy-done.5
  100.5 5.9 %slot_rows.1 = (bf16[3,64,1024]{2,1,0:T(8,128)(2,1)S(1)}, bf16[3,16,64,128]{3,2,1,0:T(8,128)(2,1)}) custom-call(s32[33]{0:T(128)} %copy-done.21, bf16[1056,128]{1,0:T(8,128)(2,1)} %copy-done.20, bf16[1056,128]{1,0:T(8,128)(2,1)} %collective-permute-done.10.refs_1_, bf16[1056,128]{1,0:T(8,128)(2,1)} %collective-permute-done.11.refs_2_, ...), custom_call_target="tpu_custom_call" | custom-call | flops 400000000 | bytes 20000000 | tf_op jit(solution)/shard_map/slot_rows/pallas_call | solution.py:350
  107.0 4.2 %project.7 = bf16[4,192,512]{2,1,0:T(8,128)(2,1)S(1)} custom-call(s32[4]{0:T(128)S(1)} %copy-done.19, bf16[192,1024]{1,0:T(8,128)(2,1)S(1)} %bitcast.47, bf16[1024,4096]{1,0:T(8,128)(2,1)} %weight.7), custom_call_target="tpu_custom_call" | custom-call | flops 805306368 | bytes 6000000 | tf_op jit(solution)/shard_map/project/pallas_call | solution.py:377
  111.3 1.6 %collective-permute-start.24 = (bf16[4,192,512]{2,1,0:T(8,128)(2,1)S(1)}, bf16[4,192,512]{2,1,0:T(8,128)(2,1)S(1)}, u32[]{:S(2)}, u32[]{:S(2)}) collective-permute-start(bf16[4,192,512]{2,1,0:T(8,128)(2,1)S(1)} %project.7), channel_id=1, source_target_pairs={{0,1},{1,0},{2,3},{3,2},{4,5},{5,4},{6,7},{7,6},{8,9},{9,8},{10,11... | collective-permute-start | bytes 2359304 | tf_op jit(solution)/shard_map/ppermute | solution.py:402
  112.9 4.4 %project.4 = bf16[4,256,512]{2,1,0:T(8,128)(2,1)S(1)} custom-call(s32[4]{0:T(128)S(1)} %broadcast_add_fusion.blocks, bf16[256,1024]{1,0:T(8,128)(2,1)S(1)} %bitcast.46, bf16[1024,4096]{1,0:T(8,128)(2,1)} %weight.7), custom_call_target="tpu_custom_call" | custom-call | flops 1073741824 | bytes 6000000 | tf_op jit(solution)/shard_map/project/pallas_call | solution.py:377
  117.3 1.3 fusion.6
  118.6 1.4 collective-permute-start.7
  120.0 2.6 %collective-permute-start.8 = (bf16[256,512]{1,0:T(8,128)(2,1)S(1)}, bf16[256,512]{1,0:T(8,128)(2,1)S(1)}, u32[]{:S(2)}, u32[]{:S(2)}) collective-permute-start(bf16[256,512]{1,0:T(8,128)(2,1)S(1)} %get-tuple-element.72), channel_id=1, source_target_pairs={{0,4},{1,5},{2,6},{3,7},{4,0},{5,1},{6,2},{7,3},{8,12},{9,13},{10,... | collective-permute-start | bytes 786440 | tf_op jit(solution)/shard_map/ppermute | solution.py:408
  122.6 1.1 collective-permute-start.9
  123.7 4.2 %project.6 = bf16[4,192,512]{2,1,0:T(8,128)(2,1)S(1)} custom-call(s32[4]{0:T(128)S(1)} %broadcast_add_fusion.blocks, bf16[192,1024]{1,0:T(8,128)(2,1)S(1)} %bitcast.48, bf16[1024,4096]{1,0:T(8,128)(2,1)} %weight.7), custom_call_target="tpu_custom_call" | custom-call | flops 805306368 | bytes 6000000 | tf_op jit(solution)/shard_map/project/pallas_call | solution.py:377
  128.6 0.8 collective-permute-start.26
  129.4 1.7 %collective-permute-start.27 = (bf16[192,512]{1,0:T(8,128)(2,1)S(1)}, bf16[192,512]{1,0:T(8,128)(2,1)S(1)}, u32[]{:S(2)}, u32[]{:S(2)}) collective-permute-start(bf16[192,512]{1,0:T(8,128)(2,1)S(1)} %get-tuple-element.74), channel_id=1, source_target_pairs={{0,6},{1,7},{2,0},{3,1},{4,2},{5,3},{6,4},{7,5},{8,14},{9,15},{10,... | collective-permute-start | bytes 589832 | tf_op jit(solution)/shard_map/ppermute | solution.py:408
  131.1 3.6 %collective-permute-done.8 = bf16[256,512]{1,0:T(8,128)(2,1)S(1)} collective-permute-done((bf16[256,512]{1,0:T(8,128)(2,1)S(1)}, bf16[256,512]{1,0:T(8,128)(2,1)S(1)}, u32[]{:S(2)}, u32[]{:S(2)}) %collective-permute-start.8) | collective-permute-done | bytes 262176 | tf_op jit(solution)/shard_map/ppermute | solution.py:408
  134.7 1.8 %fusion.2 = bf16[256,512]{1,0:T(8,128)(2,1)} fusion(bf16[256,512]{1,0:T(8,128)(2,1)S(1)} %collective-permute-done.9, bf16[256,512]{1,0:T(8,128)(2,1)S(1)} %collective-permute-done.8, bf16[256,512]{1,0:T(8,128)(2,1)S(1)} %collective-permute-done.7, bf16[4,256,512]{2,1,0:T(8,128)(2,1)} %collective-permute-done.6, bf16[4,256,512]{2,1,0:T(8,128)(2,1)S(1)} %project.4), kind=kLoop, calls=%fused_computation.3 | loop fusion | flops 1310720 | bytes 1572864 | tf_op jit(solution)/shard_map/convert_element_type | solution.py:409
  136.6 2.9 %collective-permute-done.25 = bf16[192,512]{1,0:T(8,128)(2,1)S(1)} collective-permute-done((bf16[192,512]{1,0:T(8,128)(2,1)S(1)}, bf16[192,512]{1,0:T(8,128)(2,1)S(1)}, u32[]{:S(2)}, u32[]{:S(2)}) %collective-permute-start.25) | collective-permute-done | bytes 196640 | tf_op jit(solution)/shard_map/ppermute | solution.py:408
  139.5 3.7 %collective-permute-done.26 = bf16[192,512]{1,0:T(8,128)(2,1)S(1)} collective-permute-done((bf16[192,512]{1,0:T(8,128)(2,1)S(1)}, bf16[192,512]{1,0:T(8,128)(2,1)S(1)}, u32[]{:S(2)}, u32[]{:S(2)}) %collective-permute-start.26) | collective-permute-done | bytes 196640 | tf_op jit(solution)/shard_map/ppermute | solution.py:408
  143.2 0.8 fusion.5
  (76 shorter events, 13.9 us)
Async XLA Ops:
  3.1 77.8 %copy-start.20 = (bf16[1056,128]{1,0:T(8,128)(2,1)}, bf16[1056,128]{1,0:T(8,128)(2,1)S(1)}, u32[]{:S(2)}) copy-start(bf16[1056,128]{1,0:T(8,128)(2,1)S(1)} %concatenate.10.refs_0_) | copy-start | bytes 811012
  3.1 14.8 %collective-permute-start.12 = (bf16[1056,128]{1,0:T(8,128)(2,1)S(1)}, bf16[1056,128]{1,0:T(8,128)(2,1)}, u32[]{:S(2)}, u32[]{:S(2)}) collective-permute-start(bf16[1056,128]{1,0:T(8,128)(2,1)S(1)} %concatenate.10.refs_0_), channel_id=1, source_target_pairs={{0,16},{8,24},{16,32},{24,40},{32,48},{40,56},{48,0},{56,8},{64,80... | collective-permute-start | bytes 811016 | tf_op jit(solution)/shard_map/ppermute | solution.py:414
  7.0 16.6 %collective-permute-start.13 = (bf16[1056,128]{1,0:T(8,128)(2,1)S(1)}, bf16[1056,128]{1,0:T(8,128)(2,1)}, u32[]{:S(2)}, u32[]{:S(2)}) collective-permute-start(bf16[1056,128]{1,0:T(8,128)(2,1)S(1)} %concatenate.10.refs_0_), channel_id=1, source_target_pairs={{0,48},{8,56},{16,0},{24,8},{32,16},{40,24},{48,32},{56,40},{64,11... | collective-permute-start | bytes 811016 | tf_op jit(solution)/shard_map/ppermute | solution.py:414
  10.1 24.6 %collective-permute-start.10 = (bf16[1056,128]{1,0:T(8,128)(2,1)S(1)}, bf16[1056,128]{1,0:T(8,128)(2,1)}, u32[]{:S(2)}, u32[]{:S(2)}) collective-permute-start(bf16[1056,128]{1,0:T(8,128)(2,1)S(1)} %concatenate.10.refs_0_), channel_id=1, source_target_pairs={{0,8},{8,16},{16,24},{24,32},{32,40},{40,48},{48,56},{56,0},{64,72... | collective-permute-start | bytes 811016 | tf_op jit(solution)/shard_map/ppermute | solution.py:414
  10.8 33.6 %collective-permute-start.11 = (bf16[1056,128]{1,0:T(8,128)(2,1)S(1)}, bf16[1056,128]{1,0:T(8,128)(2,1)}, u32[]{:S(2)}, u32[]{:S(2)}) collective-permute-start(bf16[1056,128]{1,0:T(8,128)(2,1)S(1)} %concatenate.10.refs_0_), channel_id=1, source_target_pairs={{0,56},{8,0},{16,8},{24,16},{32,24},{40,32},{48,40},{56,48},{64,12... | collective-permute-start | bytes 811016 | tf_op jit(solution)/shard_map/ppermute | solution.py:414
  17.9 27.2 %collective-permute-start.14 = (bf16[1056,128]{1,0:T(8,128)(2,1)}, bf16[1056,128]{1,0:T(8,128)(2,1)}, u32[]{:S(2)}, u32[]{:S(2)}) collective-permute-start(bf16[1056,128]{1,0:T(8,128)(2,1)} %collective-permute-done.12.refs_3_), channel_id=1, source_target_pairs={{0,8},{8,16},{16,24},{24,32},{32,40},{40,48},{48,56},{56,0},{64,72... | collective-permute-start | bytes 811016 | tf_op jit(solution)/shard_map/ppermute | solution.py:414
  23.6 21.6 %collective-permute-start.15 = (bf16[1056,128]{1,0:T(8,128)(2,1)}, bf16[1056,128]{1,0:T(8,128)(2,1)}, u32[]{:S(2)}, u32[]{:S(2)}) collective-permute-start(bf16[1056,128]{1,0:T(8,128)(2,1)} %collective-permute-done.13.refs_4_), channel_id=1, source_target_pairs={{0,56},{8,0},{16,8},{24,16},{32,24},{40,32},{48,40},{56,48},{64,12... | collective-permute-start | bytes 811016 | tf_op jit(solution)/shard_map/ppermute | solution.py:414
  25.5 34.2 %copy-start.8 = (f32[1,4,2,128]{3,1,2,0:T(4,128)}, f32[1,4,2,128]{3,1,2,0:T(4,128)S(1)}, u32[]{:S(2)}) copy-start(f32[1,4,2,128]{3,1,2,0:T(4,128)S(1)} %copy.43) | copy-start | bytes 12292
  30.2 50.9 %copy-start.21 = (s32[33]{0:T(128)}, s32[33]{0:T(128)S(1)}, u32[]{:S(2)}) copy-start(s32[33]{0:T(128)S(1)} %pad_add_fusion.info) | copy-start | bytes 400
  31.1 14.0 %collective-permute-start.16 = (bf16[528,128]{1,0:T(8,128)(2,1)S(1)}, bf16[528,128]{1,0:T(8,128)(2,1)}, u32[]{:S(2)}, u32[]{:S(2)}) collective-permute-start(bf16[528,128]{1,0:T(8,128)(2,1)S(1)} %slice.80), channel_id=1, source_target_pairs={{0,16},{8,24},{16,32},{24,40},{32,48},{40,56},{48,0},{56,8},{64,80... | collective-permute-start | bytes 405512 | tf_op jit(solution)/shard_map/ppermute | solution.py:414
  34.7 10.4 %collective-permute-start.17 = (bf16[528,128]{1,0:T(8,128)(2,1)S(1)}, bf16[528,128]{1,0:T(8,128)(2,1)}, u32[]{:S(2)}, u32[]{:S(2)}) collective-permute-start(bf16[528,128]{1,0:T(8,128)(2,1)S(1)} %slice.81), channel_id=1, source_target_pairs={{0,48},{8,56},{16,0},{24,8},{32,16},{40,24},{48,32},{56,40},{64,11... | collective-permute-start | bytes 405512 | tf_op jit(solution)/shard_map/ppermute | solution.py:414
  35.8 1.2 copy-start
  37.0 1.0 copy-start.1
  38.1 1.0 copy-start.2
  39.1 0.7 copy-start.6
  39.8 0.7 copy-start.10
  40.5 0.7 copy-start.12
  41.2 0.7 copy-start.14
  41.8 0.7 copy-start.16
  44.3 52.0 %copy-start.3 = (bf16[3,64,1024]{2,1,0:T(8,128)(2,1)S(1)}, bf16[3,64,1024]{2,1,0:T(8,128)(2,1)}, u32[]{:S(2)}) copy-start(bf16[3,64,1024]{2,1,0:T(8,128)(2,1)} %refs_21_.1) | copy-start | bytes 1179652
  44.3 52.0 %copy-start.4 = (bf16[3,64,1024]{2,1,0:T(8,128)(2,1)S(1)}, bf16[3,64,1024]{2,1,0:T(8,128)(2,1)}, u32[]{:S(2)}) copy-start(bf16[3,64,1024]{2,1,0:T(8,128)(2,1)} %refs_23_.1) | copy-start | bytes 1179652
  44.4 52.0 %copy-start.7 = (f32[4,1024]{1,0:T(4,128)S(1)}, f32[4,1024]{1,0:T(4,128)}, u32[]{:S(2)}) copy-start(f32[4,1024]{1,0:T(4,128)} %refs_25_.1) | copy-start | bytes 49156
  44.4 36.7 %copy-start.18 = (s32[4]{0:T(128)}, s32[4]{0:T(128)S(1)}, u32[]{:S(2)}) copy-start(s32[4]{0:T(128)S(1)} %add_subtract_fusion.blocks) | copy-start | bytes 52
  45.9 35.1 %collective-permute-start.18 = (bf16[1056,128]{1,0:T(8,128)(2,1)}, bf16[1056,128]{1,0:T(8,128)(2,1)S(1)}, u32[]{:S(2)}, u32[]{:S(2)}) collective-permute-start(bf16[1056,128]{1,0:T(8,128)(2,1)} %get-tuple-element.54), channel_id=1, source_target_pairs={{0,64},{8,72},{16,80},{24,88},{32,96},{40,104},{48,112},{56,120},{... | collective-permute-start | bytes 811016 | tf_op jit(solution)/shard_map/ppermute | solution.py:419
  47.2 33.9 %collective-permute-start.19 = (bf16[1056,128]{1,0:T(8,128)(2,1)}, bf16[1056,128]{1,0:T(8,128)(2,1)S(1)}, u32[]{:S(2)}, u32[]{:S(2)}) collective-permute-start(bf16[1056,128]{1,0:T(8,128)(2,1)} %get-tuple-element.55), channel_id=1, source_target_pairs={{0,128},{8,136},{16,144},{24,152},{32,160},{40,168},{48,176},{56,1... | collective-permute-start | bytes 811016 | tf_op jit(solution)/shard_map/ppermute | solution.py:419
  64.2 53.1 %collective-permute-start.6 = (bf16[4,256,512]{2,1,0:T(8,128)(2,1)S(1)}, bf16[4,256,512]{2,1,0:T(8,128)(2,1)}, u32[]{:S(2)}, u32[]{:S(2)}) collective-permute-start(bf16[4,256,512]{2,1,0:T(8,128)(2,1)S(1)} %project.5), channel_id=1, source_target_pairs={{0,1},{1,0},{2,3},{3,2},{4,5},{5,4},{6,7},{7,6},{8,9},{9,8},{10,11... | collective-permute-start | bytes 3145736 | tf_op jit(solution)/shard_map/ppermute | solution.py:402
  68.7 17.5 %collective-permute-start.20 = (bf16[1056,128]{1,0:T(8,128)(2,1)}, bf16[1056,128]{1,0:T(8,128)(2,1)S(1)}, u32[]{:S(2)}, u32[]{:S(2)}) collective-permute-start(bf16[1056,128]{1,0:T(8,128)(2,1)} %get-tuple-element.56), channel_id=1, source_target_pairs={{0,192},{8,200},{16,208},{24,216},{32,224},{40,232},{48,240},{56,2... | collective-permute-start | bytes 811016 | tf_op jit(solution)/shard_map/ppermute | solution.py:419
  80.9 15.0 %collective-permute-start.21 = (bf16[1056,128]{1,0:T(8,128)(2,1)}, bf16[1056,128]{1,0:T(8,128)(2,1)S(1)}, u32[]{:S(2)}, u32[]{:S(2)}) collective-permute-start(bf16[1056,128]{1,0:T(8,128)(2,1)} %get-tuple-element.57), channel_id=1, source_target_pairs={{0,64},{8,72},{16,80},{24,88},{32,96},{40,104},{48,112},{56,120},{... | collective-permute-start | bytes 811016 | tf_op jit(solution)/shard_map/ppermute | solution.py:419
  81.0 14.9 %collective-permute-start.22 = (bf16[1056,128]{1,0:T(8,128)(2,1)}, bf16[1056,128]{1,0:T(8,128)(2,1)}, u32[]{:S(2)}, u32[]{:S(2)}) collective-permute-start(bf16[1056,128]{1,0:T(8,128)(2,1)} %get-tuple-element.58), channel_id=1, source_target_pairs={{0,128},{8,136},{16,144},{24,152},{32,160},{40,168},{48,176},{56,1... | collective-permute-start | bytes 811016 | tf_op jit(solution)/shard_map/ppermute | solution.py:419
  81.1 15.2 %collective-permute-start.23 = (bf16[1056,128]{1,0:T(8,128)(2,1)}, bf16[1056,128]{1,0:T(8,128)(2,1)}, u32[]{:S(2)}, u32[]{:S(2)}) collective-permute-start(bf16[1056,128]{1,0:T(8,128)(2,1)} %get-tuple-element.59), channel_id=1, source_target_pairs={{0,192},{8,200},{16,208},{24,216},{32,224},{40,232},{48,240},{56,2... | collective-permute-start | bytes 811016 | tf_op jit(solution)/shard_map/ppermute | solution.py:419
  96.4 0.8 copy-start.5
  97.2 0.7 copy-start.9
  97.9 0.7 copy-start.11
  98.5 0.7 copy-start.13
  99.2 0.7 copy-start.15
  99.9 0.7 copy-start.17
  106.4 0.6 copy-start.19
  111.3 16.7 %collective-permute-start.24 = (bf16[4,192,512]{2,1,0:T(8,128)(2,1)S(1)}, bf16[4,192,512]{2,1,0:T(8,128)(2,1)S(1)}, u32[]{:S(2)}, u32[]{:S(2)}) collective-permute-start(bf16[4,192,512]{2,1,0:T(8,128)(2,1)S(1)} %project.7), channel_id=1, source_target_pairs={{0,1},{1,0},{2,3},{3,2},{4,5},{5,4},{6,7},{7,6},{8,9},{9,8},{10,11... | collective-permute-start | bytes 2359304 | tf_op jit(solution)/shard_map/ppermute | solution.py:402
  118.6 10.8 %collective-permute-start.7 = (bf16[256,512]{1,0:T(8,128)(2,1)S(1)}, bf16[256,512]{1,0:T(8,128)(2,1)S(1)}, u32[]{:S(2)}, u32[]{:S(2)}) collective-permute-start(bf16[256,512]{1,0:T(8,128)(2,1)S(1)} %get-tuple-element.70), channel_id=1, source_target_pairs={{0,2},{1,3},{2,4},{3,5},{4,6},{5,7},{6,0},{7,1},{8,10},{9,11},{10,... | collective-permute-start | bytes 786440 | tf_op jit(solution)/shard_map/ppermute | solution.py:408
  120.0 14.7 %collective-permute-start.8 = (bf16[256,512]{1,0:T(8,128)(2,1)S(1)}, bf16[256,512]{1,0:T(8,128)(2,1)S(1)}, u32[]{:S(2)}, u32[]{:S(2)}) collective-permute-start(bf16[256,512]{1,0:T(8,128)(2,1)S(1)} %get-tuple-element.72), channel_id=1, source_target_pairs={{0,4},{1,5},{2,6},{3,7},{4,0},{5,1},{6,2},{7,3},{8,12},{9,13},{10,... | collective-permute-start | bytes 786440 | tf_op jit(solution)/shard_map/ppermute | solution.py:408
  122.6 12.1 %collective-permute-start.9 = (bf16[256,512]{1,0:T(8,128)(2,1)S(1)}, bf16[256,512]{1,0:T(8,128)(2,1)S(1)}, u32[]{:S(2)}, u32[]{:S(2)}) collective-permute-start(bf16[256,512]{1,0:T(8,128)(2,1)S(1)} %get-tuple-element.71), channel_id=1, source_target_pairs={{0,6},{1,7},{2,0},{3,1},{4,2},{5,3},{6,4},{7,5},{8,14},{9,15},{10,... | collective-permute-start | bytes 786440 | tf_op jit(solution)/shard_map/ppermute | solution.py:408
  128.1 11.3 %collective-permute-start.25 = (bf16[192,512]{1,0:T(8,128)(2,1)S(1)}, bf16[192,512]{1,0:T(8,128)(2,1)S(1)}, u32[]{:S(2)}, u32[]{:S(2)}) collective-permute-start(bf16[192,512]{1,0:T(8,128)(2,1)S(1)} %get-tuple-element.73), channel_id=1, source_target_pairs={{0,2},{1,3},{2,4},{3,5},{4,6},{5,7},{6,0},{7,1},{8,10},{9,11},{10,... | collective-permute-start | bytes 589832 | tf_op jit(solution)/shard_map/ppermute | solution.py:408
  128.6 14.6 %collective-permute-start.26 = (bf16[192,512]{1,0:T(8,128)(2,1)S(1)}, bf16[192,512]{1,0:T(8,128)(2,1)S(1)}, u32[]{:S(2)}, u32[]{:S(2)}) collective-permute-start(bf16[192,512]{1,0:T(8,128)(2,1)S(1)} %get-tuple-element.75), channel_id=1, source_target_pairs={{0,4},{1,5},{2,6},{3,7},{4,0},{5,1},{6,2},{7,3},{8,12},{9,13},{10,... | collective-permute-start | bytes 589832 | tf_op jit(solution)/shard_map/ppermute | solution.py:408
  129.4 13.8 %collective-permute-start.27 = (bf16[192,512]{1,0:T(8,128)(2,1)S(1)}, bf16[192,512]{1,0:T(8,128)(2,1)S(1)}, u32[]{:S(2)}, u32[]{:S(2)}) collective-permute-start(bf16[192,512]{1,0:T(8,128)(2,1)S(1)} %get-tuple-element.74), channel_id=1, source_target_pairs={{0,6},{1,7},{2,0},{3,1},{4,2},{5,3},{6,4},{7,5},{8,14},{9,15},{10,... | collective-permute-start | bytes 589832 | tf_op jit(solution)/shard_map/ppermute | solution.py:408

commit v2 on v1

--- a/solution.py
+++ b/solution.py
@@ -24,7 +24,7 @@
 EARLY = (0, 1, 7, 2, 6)
 LATE = (3, 5, 4)
 ORDER = EARLY + LATE
-VMEM_LIMIT = 48 * 1024 * 1024
+VMEM_LIMIT = 58 * 1024 * 1024
 
 
 def lanes_of(shape):
@@ -35,22 +35,26 @@
     return lax.broadcasted_iota(jnp.int32, shape, 0)
 
 
-def mix_rows(win_x, win_bc, dt_pad, gated, dt, z_ref, params, load_state, store_state, out_ref):
+def mix_rows(win_x, win_bc, dt_pad, gated, dt, z_ref, params, load_state, store_state, normed, slot):
     wx, wbc, dt_bias, a_log, d_skip, norm_w = params
-    acc = win_bc[TOP - 3 : TOP - 3 + ROWS, :] * wbc[0:1, :]
-    for k in range(1, TAPS):
-        acc += win_bc[TOP - 3 + k : TOP - 3 + k + ROWS, :] * wbc[k : k + 1, :]
-    bcc = acc / (1.0 + jnp.exp(-acc))
-    coeff_b = bcc[:, :STATE].astype(BF16)
-    coeff_c = bcc[:, STATE:].astype(BF16)
-
-    raw = dt + dt_bias[...]
+    coeffs = []
+    for part in range(2):
+        cols = slice(part * STATE, part * STATE + STATE)
+        acc = win_bc[TOP - 3 : TOP - 3 + ROWS, cols] * wbc[0, part : part + 1, :]
+        for k in range(1, TAPS):
+            acc += win_bc[TOP - 3 + k : TOP - 3 + k + ROWS, cols] * wbc[k, part : part + 1, :]
+        coeffs.append((acc / (1.0 + jnp.exp(-acc))).astype(BF16))
+    coeff_b, coeff_c = coeffs
+
+    dt_pad[...] = jnp.zeros_like(dt_pad)
+    dt_pad[0:HEADS, 0:ROWS] = dt[0].astype(F32)
+    raw = dt_pad[...].T[0:ROWS, 0:HEADS] + dt_bias[...]
     step = jnp.maximum(raw, 0.0) + jnp.log(1.0 + jnp.exp(-jnp.abs(raw)))
     dt_pad[...] = jnp.zeros_like(dt_pad)
-    dt_pad[0, :, 0:HEADS] = step
-    dt_pad[1, :, 0:HEADS] = step * -jnp.exp(a_log[...])
-    size = dt_pad[0]
-    cum = dt_pad[1]
+    dt_pad[0:ROWS, 0:HEADS] = step
+    dt_pad[ROWS:, 0:HEADS] = step * -jnp.exp(a_log[...])
+    size = dt_pad[0:ROWS]
+    cum = dt_pad[ROWS:]
     row = rows_of((ROWS, 128))
     for shift in (1, 2, 4, 8, 16, 32):
         cum = cum + jnp.where(row >= shift, pltpu.roll(cum, shift, 0), 0.0)
@@ -106,39 +110,73 @@
         gated[:, cols] = g
         squares += g * g
     scale = lax.rsqrt(jnp.sum(squares, axis=1, keepdims=True) * (1.0 / INNER) + 1e-05)
-    out_ref[0] = (gated[...] * scale * norm_w[...]).astype(BF16)
+    normed[pl.ds(slot * ROWS, ROWS), :] = (gated[...] * scale * norm_w[...]).astype(BF16)
+
+
+def load_pairs(win_bc, bc):
+    both = bc[0].astype(F32)
+    win_bc[TOP:, :STATE] = both[:, 0, :]
+    win_bc[TOP:, STATE:] = both[:, 1, :]
+
+
+def project(blocks, normed, weight, sent, kept):
+    width = sent.shape[2]
+    for at, out in ((0, sent), (NY, kept)):
+        for k in range(NY):
+            start = pl.multiple_of(blocks[at + k] * width, width)
+            out[k] = jnp.dot(
+                normed[...], weight[:, pl.ds(start, width)], preferred_element_type=F32
+            ).astype(BF16)
 
 
 def resident_kernel(
-    count, state, conv_x, conv_bc, x, bc, z, dt,
-    wx, wbc, dt_bias, a_log, d_skip, norm_w, out, win_x, win_bc, dt_pad, gated,
+    count, blocks, out_w, state, conv_x, conv_bc, x, bc, z, dt,
+    wx, wbc, dt_bias, a_log, d_skip, norm_w, sent, kept, conv_rows, normed, weight,
+    weight_sem, win_x, win_bc, dt_pad, gated,
 ):
     slot = pl.program_id(0)
+    fetch = pltpu.make_async_copy(out_w, weight, weight_sem)
+
+    @pl.when(slot == 0)
+    def _():
+        fetch.start()
+        conv_rows[...] = conv_x[...].astype(F32)
 
     @pl.when(slot < count[0])
     def _():
-        win_x[TOP - 3 : TOP, :] = conv_x[0].astype(F32)
+        for k in range(TAPS - 1):
+            win_x[TOP - 3 + k : TOP - 2 + k, :] = conv_rows[k, pl.ds(slot, 1), :]
         win_x[TOP:, :] = x[0].astype(F32)
-        win_bc[TOP - 3 : TOP, :] = conv_bc[0].astype(F32)
-        win_bc[TOP:, :] = bc[0].astype(F32)
+        for k in range(TAPS - 1):
+            both = conv_bc[0, k].astype(F32)
+            for part in range(2):
+                win_bc[TOP - 3 + k : TOP - 2 + k, part * STATE : part * STATE + STATE] = both[
+                    part : part + 1
+                ]
+        load_pairs(win_bc, bc)
 
         def load_state(pair):
             return state[0, 2 * pair : 2 * pair + 2].reshape(128, STATE)
 
         mix_rows(
-            win_x, win_bc, dt_pad, gated, dt[0].astype(F32), z,
-            (wx, wbc, dt_bias, a_log, d_skip, norm_w), load_state, None, out,
+            win_x, win_bc, dt_pad, gated, dt, z,
+            (wx, wbc, dt_bias, a_log, d_skip, norm_w), load_state, None, normed, slot,
         )
 
     @pl.when(slot >= count[0])
     def _():
-        out[...] = jnp.zeros_like(out)
+        normed[pl.ds(slot * ROWS, ROWS), :] = jnp.zeros((ROWS, INNER), BF16)
+
+    @pl.when(slot == pl.num_programs(0) - 1)
+    def _():
+        fetch.wait()
+        project(blocks, normed, weight, sent, kept)
 
 
 ROW_SCRATCH = [
     pltpu.VMEM((TOP + ROWS, INNER), F32),
     pltpu.VMEM((TOP + ROWS, 2 * STATE), F32),
-    pltpu.VMEM((2, ROWS, 128), F32),
+    pltpu.VMEM((2 * ROWS, 128), F32),
     pltpu.VMEM((ROWS, INNER), F32),
 ]
 
@@ -151,23 +189,38 @@
     return pl.BlockSpec((1,) + shape, lambda i, *_: (i,) + (0,) * len(shape))
 
 
-def resident_rows(count, state, conv_x, conv_bc, x, bc, z, dt, params):
+def row_scratch(slots):
+    return [
+        pltpu.VMEM((slots * ROWS, INNER), BF16),
+        pltpu.VMEM((INNER, 4096), BF16),
+        pltpu.SemaphoreType.DMA,
+    ] + ROW_SCRATCH
+
+
+def partial_sums(slots):
+    shape = (NY, slots * ROWS, 4096 // 8)
+    return [jax.ShapeDtypeStruct(shape, BF16)] * 2
+
+
+def resident_rows(count, blocks, out_w, state, conv_x, conv_bc, x, bc, z, dt, params):
     slots = state.shape[0]
+    sums = partial_sums(slots)
     return pl.pallas_call(
         resident_kernel,
-        grid_spec=pltpu.PrefetchScalarGridSpec(
-            num_scalar_prefetch=1,
-            grid=(slots,),
-            in_specs=[per_slot(a.shape[1:]) for a in (state, conv_x, conv_bc, x, bc, z, dt)]
-            + [whole(a) for a in params],
-            out_specs=per_slot((ROWS, INNER)),
-            scratch_shapes=ROW_SCRATCH,
+        grid=(slots,),
+        in_specs=[pl.BlockSpec(memory_space=pltpu.SMEM)] * 2
+        + [pl.BlockSpec(memory_space=pl.ANY), per_slot(state.shape[1:]), whole(conv_x)]
+        + [per_slot(a.shape[1:]) for a in (conv_bc, x, bc, z, dt)]
+        + [whole(a) for a in params],
+        out_specs=[whole(a) for a in sums],
+        out_shape=sums,
+        scratch_shapes=[pltpu.VMEM((TAPS - 1, slots, INNER), F32)] + row_scratch(slots),
+        compiler_params=pltpu.CompilerParams(vmem_limit_bytes=VMEM_LIMIT),
+        cost_estimate=pl.CostEstimate(
+            flops=3_000_000_000, bytes_accessed=16_000_000, transcendentals=0
         ),
-        out_shape=jax.ShapeDtypeStruct((slots, ROWS, INNER), BF16),
-        compiler_params=pltpu.CompilerParams(vmem_limit_bytes=VMEM_LIMIT),
-        cost_estimate=pl.CostEstimate(flops=400_000_000, bytes_accessed=16_000_000, transcendentals=0),
         name="resident_rows",
-    )(count, state, conv_x, conv_bc, x, bc, z, dt, *params)
+    )(count, blocks, out_w, state, conv_x, conv_bc, x, bc, z, dt, *params)
 
 
 def line_hits(assign, target, column):
@@ -200,6 +253,18 @@
 def forward_kernel(rounds, offsets, info, *refs):
     count = len(offsets) + (1 if 4 in offsets else 0)
     ins, outs, sems = refs[:count], refs[count:-1], refs[-1]
+    halves = []
+    if 4 not in offsets:
+        halves = [
+            pltpu.make_async_copy(
+                ins[offsets.index(2)].at[pl.ds(0, HALF)], outs[-2], sems.at[NX - 1]
+            ),
+            pltpu.make_async_copy(
+                ins[offsets.index(6)].at[pl.ds(HALF, HALF)], outs[-1], sems.at[NX]
+            ),
+        ]
+    for copy in halves:
+        copy.start()
     packets, at = {}, 0
     for offset in offsets:
         if offset == 4:
@@ -233,17 +298,20 @@
         def _(copies=copies):
             for copy in copies:
                 copy.wait()
+    for copy in halves:
+        copy.wait()
 
 
 def forward(rounds, offsets, info, packets):
     count = len(rounds) * (NX - 1)
+    shapes = [(PACK, 128)] * count + ([] if 4 in offsets else [(HALF, 128)] * 2)
     return pl.pallas_call(
         functools.partial(forward_kernel, rounds, offsets),
         in_specs=[pl.BlockSpec(memory_space=pltpu.SMEM)]
         + [pl.BlockSpec(memory_space=pl.ANY)] * len(packets),
-        out_specs=[pl.BlockSpec(memory_space=pl.ANY)] * count,
-        out_shape=[jax.ShapeDtypeStruct((PACK, 128), BF16)] * count,
-        scratch_shapes=[pltpu.SemaphoreType.DMA((count,))],
+        out_specs=[pl.BlockSpec(memory_space=pl.ANY)] * len(shapes),
+        out_shape=[jax.ShapeDtypeStruct(shape, BF16) for shape in shapes],
+        scratch_shapes=[pltpu.SemaphoreType.DMA((len(shapes),))],
         cost_estimate=pl.CostEstimate(flops=0, bytes_accessed=3_000_000, transcendentals=0),
         name="forward",
     )(info, *packets)
@@ -267,11 +335,12 @@
 ARRIVED = 4 * (NX - 1)
 
 
-def slot_kernel(info, *refs):
+def slot_kernel(info, blocks, out_w, *refs):
     line, rest = refs[:PACKETS], refs[PACKETS:]
     came, rest = rest[:ARRIVED], rest[ARRIVED:]
-    (x, bc, z, dt, wx, wbc, dt_bias, a_log, d_skip, norm_w, out, state,
-     held, valid, win_x, win_bc, dt_pad, gated, sems) = rest
+    (x, bc, z, dt, wx, wbc, dt_bias, a_log, d_skip, norm_w, sent, kept, state,
+     held, valid, sems, normed, weight, weight_sem, win_x, win_bc, dt_pad, gated) = rest
+    fetch = pltpu.make_async_copy(out_w, weight, weight_sem)
     packets = {o: line[i] for i, o in enumerate(ORDER[:-1])}
     packets[4] = (line[PACKETS - 2], line[PACKETS - 1])
     slot = pl.program_id(0)
@@ -281,21 +350,17 @@
     @pl.when(slot == 0)
     def _():
         before = jnp.int32(0)
-        order = []
         for request in range(NX * NZ):
-            mine = (info[request] == me).astype(jnp.int32)
-            order.append(before)
-            before = before + mine
-        valid[0] = before
+            valid[request] = before
+            before = before + (info[request] == me).astype(jnp.int32)
+        valid[NX * NZ] = before
         for shift in range(NX):
             sender = lax.rem(column + NX - shift, NX)
             hits = line_hits(info, me, sender)
             ranks = round_ranks(hits)
             for offset, hit, rank in zip(ORDER, hits, ranks):
                 source = sender * NZ + lax.rem(my_z + NZ - offset, NZ)
-                place = jnp.int32(0)
-                for request in range(NX * NZ):
-                    place = jnp.where(source == request, order[request], place)
+                place = valid[source]
 
                 @pl.when(hit == 1)
                 def _(shift=shift, offset=offset, rank=rank, place=place):
@@ -309,13 +374,14 @@
                                 pltpu.make_async_copy(
                                     came[n * (NX - 1) + shift - 1], held.at[place], sems.at[place]
                                 ).start()
-
-    live = slot < valid[0]
+        fetch.start()
+
+    live = slot < valid[NX * NZ]
 
     @pl.when(live)
     def _():
         win_x[TOP:, :] = x[0].astype(F32)
-        win_bc[TOP:, :] = bc[0].astype(F32)
+        load_pairs(win_bc, bc)
         pltpu.make_async_copy(held.at[slot], held.at[slot], sems.at[slot]).wait()
         conv = held[slot, 1024:PACK, :].astype(F32)
         for k in range(TAPS - 1):
@@ -335,73 +401,56 @@
             state[0, 2 * pair : 2 * pair + 2] = value.astype(BF16).reshape(2, 64, STATE)
 
         mix_rows(
-            win_x, win_bc, dt_pad, gated, dt[0].astype(F32), z,
-            (wx, wbc, dt_bias, a_log, d_skip, norm_w), load_state, store_state, out,
+            win_x, win_bc, dt_pad, gated, dt, z,
+            (wx, wbc, dt_bias, a_log, d_skip, norm_w), load_state, store_state, normed, slot,
         )
 
     @pl.when(jnp.logical_not(live))
     def _():
-        out[...] = jnp.zeros_like(out)
+        normed[pl.ds(slot * ROWS, ROWS), :] = jnp.zeros((ROWS, INNER), BF16)
         state[...] = jnp.zeros_like(state)
 
-
-def slot_rows(info, line, came, x, bc, z, dt, params):
+    @pl.when(slot == pl.num_programs(0) - 1)
+    def _():
+        fetch.wait()
+        project(blocks, normed, weight, sent, kept)
+
+
+def slot_rows(info, blocks, out_w, line, came, x, bc, z, dt, params):
     slots = x.shape[0]
+    sums = partial_sums(slots)
     return pl.pallas_call(
         slot_kernel,
         grid=(slots,),
-        in_specs=[pl.BlockSpec(memory_space=pltpu.SMEM)]
-        + [pl.BlockSpec(memory_space=pl.ANY)] * (PACKETS + ARRIVED)
+        in_specs=[pl.BlockSpec(memory_space=pltpu.SMEM)] * 2
+        + [pl.BlockSpec(memory_space=pl.ANY)] * (1 + PACKETS + ARRIVED)
         + [per_slot(a.shape[1:]) for a in (x, bc, z, dt)]
         + [whole(a) for a in params],
-        out_specs=[per_slot((ROWS, INNER)), per_slot((HEADS, 64, STATE))],
-        out_shape=[
-            jax.ShapeDtypeStruct((slots, ROWS, INNER), BF16),
-            jax.ShapeDtypeStruct((slots, HEADS, 64, STATE), BF16),
-        ],
-        scratch_shapes=[pltpu.VMEM((CAP, PACK, 128), BF16), pltpu.SMEM((1,), jnp.int32)]
-        + ROW_SCRATCH
-        + [pltpu.SemaphoreType.DMA((CAP,))],
-        compiler_params=pltpu.CompilerParams(vmem_limit_bytes=VMEM_LIMIT),
-        cost_estimate=pl.CostEstimate(flops=400_000_000, bytes_accessed=20_000_000, transcendentals=0),
-        name="slot_rows",
-    )(info, *line, *came, x, bc, z, dt, *params)
-
-
-def project_kernel(blocks, rows, weight, out):
-    out[0] = jnp.dot(rows[...], weight[...], preferred_element_type=F32).astype(BF16)
-
-
-def project(blocks, rows, weight):
-    count, width = blocks.shape[0], weight.shape[1] // 8
-    return pl.pallas_call(
-        project_kernel,
-        grid_spec=pltpu.PrefetchScalarGridSpec(
-            num_scalar_prefetch=1,
-            grid=(count,),
-            in_specs=[
-                pl.BlockSpec(rows.shape, lambda i, blocks: (0, 0)),
-                pl.BlockSpec((weight.shape[0], width), lambda i, blocks: (0, blocks[i])),
-            ],
-            out_specs=pl.BlockSpec((1, rows.shape[0], width), lambda i, blocks: (i, 0, 0)),
-        ),
-        out_shape=jax.ShapeDtypeStruct((count, rows.shape[0], width), BF16),
+        out_specs=[whole(a) for a in sums] + [per_slot((HEADS, 64, STATE))],
+        out_shape=sums + [jax.ShapeDtypeStruct((slots, HEADS, 64, STATE), BF16)],
+        scratch_shapes=[
+            pltpu.VMEM((CAP, PACK, 128), BF16),
+            pltpu.SMEM((NX * NZ + 1,), jnp.int32),
+            pltpu.SemaphoreType.DMA((CAP,)),
+        ]
+        + row_scratch(slots),
         compiler_params=pltpu.CompilerParams(vmem_limit_bytes=VMEM_LIMIT),
         cost_estimate=pl.CostEstimate(
-            flops=2 * count * rows.shape[0] * weight.shape[0] * width,
-            bytes_accessed=6_000_000, transcendentals=0,
+            flops=3_000_000_000, bytes_accessed=20_000_000, transcendentals=0
         ),
-        name="project",
-    )(blocks, rows, weight)
-
-
-def reduce_out(normed, out_w, sent, kept):
-    slots = normed.shape[0]
-    rows = normed.reshape(slots * ROWS, INNER)
-    mates = [(t, t ^ 1) for t in range(2 * NY)]
-    from_mate = lax.ppermute(project(sent, rows, out_w), "tp", mates)
-    own = project(kept, rows, out_w)
-    chip = [own[k].astype(F32) + from_mate[k].astype(F32) for k in range(NY)]
+        name="slot_rows",
+    )(info, blocks, out_w, *line, *came, x, bc, z, dt, *params)
+
+
+def across_cores(array):
+    return lax.ppermute(array, "tp", [(t, t ^ 1) for t in range(2 * NY)])
+
+
+def chip_sums(own, from_mate):
+    return [own[k].astype(F32) + from_mate[k].astype(F32) for k in range(NY)]
+
+
+def reduce_out(chip, slots):
     total = chip[0]
     for k in range(1, NY):
         shifted = [(t, (t + 2 * k) % (2 * NY)) for t in range(2 * NY)]
@@ -445,24 +494,32 @@
     up2, down2 = along_z(packet, 2), along_z(packet, -2)
 
     params = (
-        conv_wx, conv_wbc.reshape(TAPS, 2 * STATE), dt_bias[None], a_log[None], d_skip[None],
+        conv_wx, conv_wbc, dt_bias[None], a_log[None], d_skip[None],
         norm_w[None],
-    )
-    res_normed = resident_rows(
-        res_count, res_state, res_conv_x, res_conv_bc.reshape(-1, TAPS - 1, 2 * STATE), res_x,
-        res_bc.reshape(-1, ROWS, 2 * STATE), res_z, res_dt, params,
     )
     chip, core = tp // 2, tp % 2
     turns = (chip + jnp.arange(NY, dtype=jnp.int32)) % NY
-    sent, kept = 2 * turns + 1 - core, 2 * turns + core
+    blocks = jnp.concatenate([2 * turns + 1 - core, 2 * turns + core])
+    res_sent, res_kept = resident_rows(
+        res_count, blocks, out_w, res_state, res_conv_x.transpose(1, 0, 2),
+        res_conv_bc, res_x, res_bc, res_z, res_dt.transpose(0, 2, 1), params,
+    )
+    up1, down1, up2, down2, res_sent, res_kept = lax.optimization_barrier(
+        (up1, down1, up2, down2, res_sent, res_kept)
+    )
 
     early = [packet, up1, down1, up2, down2]
-    first = along_x(forward((0,), EARLY, info, early))
+    *ahead, up2_half, down2_half = forward((0,), EARLY, info, early)
+    up4, down4 = along_z(up2_half, 2), along_z(down2_half, -2)
     up3, down3 = along_z(up2, 1), along_z(down2, -1)
-    up4, down4 = along_z(up2[:HALF], 2), along_z(down2[HALF:], -2)
+    first = along_x(ahead)
+    res_mate = across_cores(res_sent)
+    up3, down3, up4, down4, *first = lax.optimization_barrier((up3, down3, up4, down4, *first))
     line = early + [up3, down3, up4, down4]
-    res_out = reduce_out(res_normed, out_w, sent, kept)
-    second = along_x(forward((1,), ORDER, info, line))
+    ahead = forward((1,), ORDER, info, line)
+    *ahead, info, res_mate, res_kept = lax.optimization_barrier((*ahead, info, res_mate, res_kept))
+    second = along_x(ahead)
+    res_chip = chip_sums(res_kept, res_mate)
 
     ids = jnp.arange(NX * NZ)
     goes = assignment[None, :] == ids[:, None]
@@ -478,11 +535,13 @@
         lambda *held: tuple(blank(held[0], 2 * (NX - 1))),
         info, *line,
     )
-    slot_normed, slot_state = slot_rows(
-        info, line, first + second + list(third), slot_x,
-        slot_bc.reshape(-1, ROWS, 2 * STATE), slot_z, slot_dt, params,
-    )
-    slot_out = reduce_out(slot_normed, out_w, sent, kept)
+    res_out = reduce_out(res_chip, res_state.shape[0])
+    *second, res_out = lax.optimization_barrier((*second, res_out))
+    sent, kept, slot_state = slot_rows(
+        info, blocks, out_w, line, first + second + list(third), slot_x, slot_bc, slot_z,
+        slot_dt.transpose(0, 2, 1), params,
+    )
+    slot_out = reduce_out(chip_sums(kept, across_cores(sent)), slot_x.shape[0])
     return res_out, slot_out, slot_state
 
 

time: 146 us -> 115 us (0.79)
  the two profiles are of different devices: /device:TPU:1 before, /device:TPU:38 now
where the time goes in v2:
time: 115 us
  waiting for transfers between devices  46.2 us (40%)
  starting transfers between devices  33.5 us (29%)
  Pallas kernels  21.4 us (19%)
  other arithmetic  8.41 us (7%)
  local copies, waits for them, and re-layouts  3.27 us (3%)
  between operations  2.07 us (2%)
    ppermute x8, starting transfers between devices, along_z(): return lax.ppermute(array, 'rep', pairs)  15.1 us
    ppermute x6, waiting for transfers between devices, reduce_out(): lax.ppermute(chip[k].astype(BF16), 'tp', shifted).astype(F32)  14.8 us
    ppermute x8, waiting for transfers between devices, along_z(): return lax.ppermute(array, 'rep', pairs)  14.8 us
    ppermute x6, waiting for transfers between devices, along_x(): lax.ppermute(array, 'rep', [(x * NZ + z, (x + shift) % NX * NZ + z) for x...  14.1 us
    ppermute x6, starting transfers between devices, reduce_out(): lax.ppermute(chip[k].astype(BF16), 'tp', shifted).astype(F32)  11.6 us
    pallas_call x1, Pallas kernels, resident_rows(): pl.pallas_call(resident_kernel, grid=(slots,), in_specs=[pl.BlockSpec(mem...  10.4 us
    pallas_call x1, Pallas kernels, slot_rows(): pl.pallas_call(slot_kernel, grid=(slots,), in_specs=[pl.BlockSpec(memory_...  8.31 us
    ppermute x6, starting transfers between devices, along_x(): lax.ppermute(array, 'rep', [(x * NZ + z, (x + shift) % NX * NZ + z) for x...  6.72 us
  transfers between devices with their start and end apart: 22, of which 14 were waited for; matrix products, arithmetic and copies ran while one was open for 3% of the time, Pallas kernels for 11%

profile of v2, /device:TPU:38, one launch (start us, length us, event | category | flops | bytes accessed | tf_op | source)
XLA Modules:
  0.0 114.8 jit_solution(11497638836445518152)
XLA Ops:
  0.6 0.7 reshape.120
  1.3 0.7 reshape.119
  2.1 1.0 concatenate.10.refs_0_
  3.1 5.5 %collective-permute-start.9 = (bf16[1056,128]{1,0:T(8,128)(2,1)S(1)}, bf16[1056,128]{1,0:T(8,128)(2,1)S(1)}, u32[]{:S(2)}, u32[]{:S(2)}) collective-permute-start(bf16[1056,128]{1,0:T(8,128)(2,1)S(1)} %concatenate.10.refs_0_), channel_id=1, source_target_pairs={{0,48},{8,56},{16,0},{24,8},{32,16},{40,24},{48,32},{56,40},{64,11... | collective-permute-start | bytes 811016 | tf_op jit(solution)/shard_map/ppermute | solution.py:463
  8.6 1.0 collective-permute-start.7
  9.6 1.0 collective-permute-start.6
  11.3 0.6 pad_add_fusion.1.blocks
  11.9 10.4 %resident_rows.1 = (bf16[4,256,512]{2,1,0:T(8,128)(2,1)}, bf16[4,256,512]{2,1,0:T(8,128)(2,1)}) custom-call(s32[1]{0:T(128)S(6)} %copy.38.count, s32[8]{0:T(128)} %pad_add_fusion.1.blocks, bf16[1024,4096]{1,0:T(8,128)(2,1)} %out_w.3, bf16[4,16,64,128]{3,2,1,0:T(8,128)(2,1)} %state.1, bf16[3,4,1024]{2,1,0:T(4,128)(2,1)} %bitcast.51, ...), custom_call_target="tpu_custom_call" | custom-call | flops 3000000000 | bytes 16000000 | tf_op jit(solution)/shard_map/resident_rows/pallas_call | solution.py:208
  22.4 2.5 %collective-permute-done.8.refs_3_ = bf16[1056,128]{1,0:T(8,128)(2,1)S(1)} collective-permute-done((bf16[1056,128]{1,0:T(8,128)(2,1)S(1)}, bf16[1056,128]{1,0:T(8,128)(2,1)S(1)}, u32[]{:S(2)}, u32[]{:S(2)}) %collective-permute-start.8) | collective-permute-done | bytes 270368 | tf_op jit(solution)/shard_map/ppermute | solution.py:463
  24.9 2.5 %collective-permute-done.6.refs_1_ = bf16[1056,128]{1,0:T(8,128)(2,1)S(1)} collective-permute-done((bf16[1056,128]{1,0:T(8,128)(2,1)S(1)}, bf16[1056,128]{1,0:T(8,128)(2,1)S(1)}, u32[]{:S(2)}, u32[]{:S(2)}) %collective-permute-start.6) | collective-permute-done | bytes 270368 | tf_op jit(solution)/shard_map/ppermute | solution.py:463
  27.4 1.0 collective-permute-start.10
  28.5 1.3 %forward.4 = (bf16[1056,128]{1,0:T(8,128)(2,1)}, bf16[1056,128]{1,0:T(8,128)(2,1)}, bf16[1056,128]{1,0:T(8,128)(2,1)}, bf16[528,128]{1,0:T(8,128)(2,1)}, bf16[528,128]{1,0:T(8,128)(2,1)}) custom-call(s32[33]{0:T(128)S(1)} %pad_add_fusion.info, bf16[1056,128]{1,0:T(8,128)(2,1)S(1)} %concatenate.10.refs_0_, ...), custom_call_target="tpu_custom_call" | custom-call | bytes 3000000 | tf_op jit(solution)/shard_map/forward/pallas_call | solution.py:308
  29.8 3.0 %collective-permute-start.12 = (bf16[528,128]{1,0:T(8,128)(2,1)}, bf16[528,128]{1,0:T(8,128)(2,1)S(1)}, u32[]{:S(2)}, u32[]{:S(2)}) collective-permute-start(bf16[528,128]{1,0:T(8,128)(2,1)} %get-tuple-element.88), channel_id=1, source_target_pairs={{0,16},{8,24},{16,32},{24,40},{32,48},{40,56},{48,0},{56,8},{64,80... | collective-permute-start | bytes 405512 | tf_op jit(solution)/shard_map/ppermute | solution.py:463
  32.8 2.2 %collective-permute-start.13 = (bf16[528,128]{1,0:T(8,128)(2,1)}, bf16[528,128]{1,0:T(8,128)(2,1)S(1)}, u32[]{:S(2)}, u32[]{:S(2)}) collective-permute-start(bf16[528,128]{1,0:T(8,128)(2,1)} %get-tuple-element.89), channel_id=1, source_target_pairs={{0,48},{8,56},{16,0},{24,8},{32,16},{40,24},{48,32},{56,40},{64,11... | collective-permute-start | bytes 405512 | tf_op jit(solution)/shard_map/ppermute | solution.py:463
  35.0 1.4 %collective-permute-start.11 = (bf16[1056,128]{1,0:T(8,128)(2,1)S(1)}, bf16[1056,128]{1,0:T(8,128)(2,1)S(1)}, u32[]{:S(2)}, u32[]{:S(2)}) collective-permute-start(bf16[1056,128]{1,0:T(8,128)(2,1)S(1)} %collective-permute-done.9.refs_4_), channel_id=1, source_target_pairs={{0,56},{8,0},{16,8},{24,16},{32,24},{40,32},{48,40},{56,48},{64,12... | collective-permute-start | bytes 811016 | tf_op jit(solution)/shard_map/ppermute | solution.py:463
  36.4 9.7 %collective-permute-done.12.refs_7_ = bf16[528,128]{1,0:T(8,128)(2,1)S(1)} collective-permute-done((bf16[528,128]{1,0:T(8,128)(2,1)}, bf16[528,128]{1,0:T(8,128)(2,1)S(1)}, u32[]{:S(2)}, u32[]{:S(2)}) %collective-permute-start.12) | collective-permute-done | bytes 135200 | tf_op jit(solution)/shard_map/ppermute | solution.py:463
  46.1 0.5 collective-permute-start.14
  46.6 2.4 %collective-permute-start.15 = (bf16[1056,128]{1,0:T(8,128)(2,1)}, bf16[1056,128]{1,0:T(8,128)(2,1)}, u32[]{:S(2)}, u32[]{:S(2)}) collective-permute-start(bf16[1056,128]{1,0:T(8,128)(2,1)} %get-tuple-element.91), channel_id=1, source_target_pairs={{0,128},{8,136},{16,144},{24,152},{32,160},{40,168},{48,176},{56,1... | collective-permute-start | bytes 811016 | tf_op jit(solution)/shard_map/ppermute | solution.py:468
  49.2 0.6 fusion.18
  50.5 5.2 %collective-permute-done.14.refs_9_ = bf16[1056,128]{1,0:T(8,128)(2,1)S(1)} collective-permute-done((bf16[1056,128]{1,0:T(8,128)(2,1)}, bf16[1056,128]{1,0:T(8,128)(2,1)S(1)}, u32[]{:S(2)}, u32[]{:S(2)}) %collective-permute-start.14) | collective-permute-done | bytes 270368 | tf_op jit(solution)/shard_map/ppermute | solution.py:468
  55.7 2.2 %collective-permute-done.15.refs_10_ = bf16[1056,128]{1,0:T(8,128)(2,1)} collective-permute-done((bf16[1056,128]{1,0:T(8,128)(2,1)}, bf16[1056,128]{1,0:T(8,128)(2,1)}, u32[]{:S(2)}, u32[]{:S(2)}) %collective-permute-start.15) | collective-permute-done | bytes 270368 | tf_op jit(solution)/shard_map/ppermute | solution.py:468
  57.9 4.2 %collective-permute-done.16.refs_11_ = bf16[1056,128]{1,0:T(8,128)(2,1)} collective-permute-done((bf16[1056,128]{1,0:T(8,128)(2,1)}, bf16[1056,128]{1,0:T(8,128)(2,1)}, u32[]{:S(2)}, u32[]{:S(2)}) %collective-permute-start.16) | collective-permute-done | bytes 270368 | tf_op jit(solution)/shard_map/ppermute | solution.py:468
  62.0 0.8 forward.5
  62.8 2.1 %fusion.6 = (bf16[256,512]{1,0:T(8,128)(2,1)}, bf16[256,512]{1,0:T(8,128)(2,1)}, bf16[256,512]{1,0:T(8,128)(2,1)}) fusion(bf16[4,256,512]{2,1,0:T(8,128)(2,1)S(1)} %collective-permute-done.17, bf16[4,256,512]{2,1,0:T(8,128)(2,1)} %get-tuple-element.105), kind=kLoop, calls=%fused_computation.14 | loop fusion | flops 1572864 | bytes 2359296 | tf_op jit(solution)/shard_map/convert_element_type | solution.py:457
  64.9 0.5 conditional.1
  64.9 0.5 blank.1
  65.5 1.7 %collective-permute-start.21 = (bf16[256,512]{1,0:T(8,128)(2,1)}, bf16[256,512]{1,0:T(8,128)(2,1)S(1)}, u32[]{:S(2)}, u32[]{:S(2)}) collective-permute-start(bf16[256,512]{1,0:T(8,128)(2,1)} %get-tuple-element.126), channel_id=1, source_target_pairs={{0,2},{1,3},{2,4},{3,5},{4,6},{5,7},{6,0},{7,1},{8,10},{9,11},{10,... | collective-permute-start | bytes 786440 | tf_op jit(solution)/shard_map/ppermute | solution.py:457
  67.2 1.7 %collective-permute-start.23 = (bf16[256,512]{1,0:T(8,128)(2,1)}, bf16[256,512]{1,0:T(8,128)(2,1)S(1)}, u32[]{:S(2)}, u32[]{:S(2)}) collective-permute-start(bf16[256,512]{1,0:T(8,128)(2,1)} %get-tuple-element.127), channel_id=1, source_target_pairs={{0,6},{1,7},{2,0},{3,1},{4,2},{5,3},{6,4},{7,5},{8,14},{9,15},{10,... | collective-permute-start | bytes 786440 | tf_op jit(solution)/shard_map/ppermute | solution.py:457
  68.8 2.0 %collective-permute-start.22 = (bf16[256,512]{1,0:T(8,128)(2,1)}, bf16[256,512]{1,0:T(8,128)(2,1)S(1)}, u32[]{:S(2)}, u32[]{:S(2)}) collective-permute-start(bf16[256,512]{1,0:T(8,128)(2,1)} %get-tuple-element.128), channel_id=1, source_target_pairs={{0,4},{1,5},{2,6},{3,7},{4,0},{5,1},{6,2},{7,3},{8,12},{9,13},{10,... | collective-permute-start | bytes 786440 | tf_op jit(solution)/shard_map/ppermute | solution.py:457
  70.8 1.0 collective-permute-start.18
  71.8 2.1 %collective-permute-start.19 = (bf16[1056,128]{1,0:T(8,128)(2,1)}, bf16[1056,128]{1,0:T(8,128)(2,1)S(1)}, u32[]{:S(2)}, u32[]{:S(2)}) collective-permute-start(bf16[1056,128]{1,0:T(8,128)(2,1)} %get-tuple-element.103), channel_id=1, source_target_pairs={{0,128},{8,136},{16,144},{24,152},{32,160},{40,168},{48,176},{56,1... | collective-permute-start | bytes 811016 | tf_op jit(solution)/shard_map/ppermute | solution.py:468
  73.8 1.5 %collective-permute-done.21 = bf16[256,512]{1,0:T(8,128)(2,1)S(1)} collective-permute-done((bf16[256,512]{1,0:T(8,128)(2,1)}, bf16[256,512]{1,0:T(8,128)(2,1)S(1)}, u32[]{:S(2)}, u32[]{:S(2)}) %collective-permute-start.21) | collective-permute-done | bytes 262176 | tf_op jit(solution)/shard_map/ppermute | solution.py:457
  75.3 0.8 collective-permute-start.20
  76.1 4.3 %collective-permute-done.23 = bf16[256,512]{1,0:T(8,128)(2,1)S(1)} collective-permute-done((bf16[256,512]{1,0:T(8,128)(2,1)}, bf16[256,512]{1,0:T(8,128)(2,1)S(1)}, u32[]{:S(2)}, u32[]{:S(2)}) %collective-permute-start.23) | collective-permute-done | bytes 262176 | tf_op jit(solution)/shard_map/ppermute | solution.py:457
  80.4 1.7 %collective-permute-done.22 = bf16[256,512]{1,0:T(8,128)(2,1)S(1)} collective-permute-done((bf16[256,512]{1,0:T(8,128)(2,1)}, bf16[256,512]{1,0:T(8,128)(2,1)S(1)}, u32[]{:S(2)}, u32[]{:S(2)}) %collective-permute-start.22) | collective-permute-done | bytes 262176 | tf_op jit(solution)/shard_map/ppermute | solution.py:457
  82.1 1.8 %fusion.2 = bf16[256,512]{1,0:T(8,128)(2,1)} fusion(bf16[256,512]{1,0:T(8,128)(2,1)S(1)} %collective-permute-done.23, bf16[256,512]{1,0:T(8,128)(2,1)S(1)} %collective-permute-done.22, bf16[256,512]{1,0:T(8,128)(2,1)S(1)} %collective-permute-done.21, bf16[4,256,512]{2,1,0:T(8,128)(2,1)S(1)} %collective-permute-done.17, bf16[4,256,512]{2,1,0:T(8,128)(2,1)} %get-tuple-element.105), kind=kLoop, calls=%fused_computation.3 | loop fusion | flops 1310720 | bytes 1572864 | tf_op jit(solution)/shard_map/convert_element_type | solution.py:458
  83.9 2.6 %collective-permute-done.20.refs_14_ = bf16[1056,128]{1,0:T(8,128)(2,1)S(1)} collective-permute-done((bf16[1056,128]{1,0:T(8,128)(2,1)}, bf16[1056,128]{1,0:T(8,128)(2,1)S(1)}, u32[]{:S(2)}, u32[]{:S(2)}) %collective-permute-start.20) | collective-permute-done | bytes 270368 | tf_op jit(solution)/shard_map/ppermute | solution.py:468
  86.5 0.7 copy-done.3
  87.2 8.3 %slot_rows.1 = (bf16[4,192,512]{2,1,0:T(8,128)(2,1)}, bf16[4,192,512]{2,1,0:T(8,128)(2,1)}, bf16[3,16,64,128]{3,2,1,0:T(8,128)(2,1)}) custom-call(s32[33]{0:T(128)S(1)} %pad_add_fusion.info, s32[8]{0:T(128)} %pad_add_fusion.1.blocks, bf16[1024,4096]{1,0:T(8,128)(2,1)} %out_w.3, bf16[1056,128]{1,0:T(8,128)(2,1)S(1)} %concatenate.10.refs_0_, ...), custom_call_target="tpu_custom_call" | custom-call | flops 3000000000 | bytes 20000000 | tf_op jit(solution)/shard_map/slot_rows/pallas_call | solution.py:422
  95.7 2.5 %collective-permute-done.24 = bf16[4,192,512]{2,1,0:T(8,128)(2,1)S(1)} collective-permute-done((bf16[4,192,512]{2,1,0:T(8,128)(2,1)}, bf16[4,192,512]{2,1,0:T(8,128)(2,1)S(1)}, u32[]{:S(2)}, u32[]{:S(2)}) %collective-permute-start.24) | collective-permute-done | bytes 786464 | tf_op jit(solution)/shard_map/ppermute | solution.py:446
  98.1 1.3 %fusion.9 = (bf16[192,512]{1,0:T(8,128)(2,1)S(1)}, bf16[192,512]{1,0:T(8,128)(2,1)S(1)}, bf16[192,512]{1,0:T(8,128)(2,1)S(1)}) fusion(bf16[4,192,512]{2,1,0:T(8,128)(2,1)S(1)} %collective-permute-done.24, bf16[4,192,512]{2,1,0:T(8,128)(2,1)} %get-tuple-element.121), kind=kLoop, calls=%fused_computation.17 | loop fusion | flops 1179648 | bytes 1769472 | tf_op jit(solution)/shard_map/convert_element_type | solution.py:457
  99.4 0.5 collective-permute-start.25
  99.9 2.8 %collective-permute-start.27 = (bf16[192,512]{1,0:T(8,128)(2,1)S(1)}, bf16[192,512]{1,0:T(8,128)(2,1)S(1)}, u32[]{:S(2)}, u32[]{:S(2)}) collective-permute-start(bf16[192,512]{1,0:T(8,128)(2,1)S(1)} %get-tuple-element.130), channel_id=1, source_target_pairs={{0,6},{1,7},{2,0},{3,1},{4,2},{5,3},{6,4},{7,5},{8,14},{9,15},{10,... | collective-permute-start | bytes 589832 | tf_op jit(solution)/shard_map/ppermute | solution.py:457
  102.7 3.0 %collective-permute-start.26 = (bf16[192,512]{1,0:T(8,128)(2,1)S(1)}, bf16[192,512]{1,0:T(8,128)(2,1)S(1)}, u32[]{:S(2)}, u32[]{:S(2)}) collective-permute-start(bf16[192,512]{1,0:T(8,128)(2,1)S(1)} %get-tuple-element.131), channel_id=1, source_target_pairs={{0,4},{1,5},{2,6},{3,7},{4,0},{5,1},{6,2},{7,3},{8,12},{9,13},{10,... | collective-permute-start | bytes 589832 | tf_op jit(solution)/shard_map/ppermute | solution.py:457
  105.7 1.9 %collective-permute-done.25 = bf16[192,512]{1,0:T(8,128)(2,1)S(1)} collective-permute-done((bf16[192,512]{1,0:T(8,128)(2,1)S(1)}, bf16[192,512]{1,0:T(8,128)(2,1)S(1)}, u32[]{:S(2)}, u32[]{:S(2)}) %collective-permute-start.25) | collective-permute-done | bytes 196640 | tf_op jit(solution)/shard_map/ppermute | solution.py:457
  107.6 1.7 %collective-permute-done.27 = bf16[192,512]{1,0:T(8,128)(2,1)S(1)} collective-permute-done((bf16[192,512]{1,0:T(8,128)(2,1)S(1)}, bf16[192,512]{1,0:T(8,128)(2,1)S(1)}, u32[]{:S(2)}, u32[]{:S(2)}) %collective-permute-start.27) | collective-permute-done | bytes 196640 | tf_op jit(solution)/shard_map/ppermute | solution.py:457
  109.3 3.7 %collective-permute-done.26 = bf16[192,512]{1,0:T(8,128)(2,1)S(1)} collective-permute-done((bf16[192,512]{1,0:T(8,128)(2,1)S(1)}, bf16[192,512]{1,0:T(8,128)(2,1)S(1)}, u32[]{:S(2)}, u32[]{:S(2)}) %collective-permute-start.26) | collective-permute-done | bytes 196640 | tf_op jit(solution)/shard_map/ppermute | solution.py:457
  113.1 1.7 %fusion.5 = bf16[192,512]{1,0:T(8,128)(2,1)} fusion(bf16[192,512]{1,0:T(8,128)(2,1)S(1)} %collective-permute-done.27, bf16[192,512]{1,0:T(8,128)(2,1)S(1)} %collective-permute-done.26, bf16[192,512]{1,0:T(8,128)(2,1)S(1)} %collective-permute-done.25, bf16[4,192,512]{2,1,0:T(8,128)(2,1)S(1)} %collective-permute-done.24, ...), kind=kLoop, calls=%fused_computation.10 | loop fusion | flops 983040 | bytes 1179648 | tf_op jit(solution)/shard_map/convert_element_type | solution.py:458
  (28 shorter events, 0.4 us)
Async XLA Ops:
  0.6 27.8 %copy-start.4 = (s32[32]{0:T(128)S(1)}, s32[32]{0:T(128)}, u32[]{:S(2)}) copy-start(s32[32]{0:T(128)} %param.40) | copy-start | bytes 388
  3.1 19.3 %collective-permute-start.9 = (bf16[1056,128]{1,0:T(8,128)(2,1)S(1)}, bf16[1056,128]{1,0:T(8,128)(2,1)S(1)}, u32[]{:S(2)}, u32[]{:S(2)}) collective-permute-start(bf16[1056,128]{1,0:T(8,128)(2,1)S(1)} %concatenate.10.refs_0_), channel_id=1, source_target_pairs={{0,48},{8,56},{16,0},{24,8},{32,16},{40,24},{48,32},{56,40},{64,11... | collective-permute-start | bytes 811016 | tf_op jit(solution)/shard_map/ppermute | solution.py:463
  8.6 16.3 %collective-permute-start.8 = (bf16[1056,128]{1,0:T(8,128)(2,1)S(1)}, bf16[1056,128]{1,0:T(8,128)(2,1)S(1)}, u32[]{:S(2)}, u32[]{:S(2)}) collective-permute-start(bf16[1056,128]{1,0:T(8,128)(2,1)S(1)} %concatenate.10.refs_0_), channel_id=1, source_target_pairs={{0,16},{8,24},{16,32},{24,40},{32,48},{40,56},{48,0},{56,8},{64,80... | collective-permute-start | bytes 811016 | tf_op jit(solution)/shard_map/ppermute | solution.py:463
  8.6 16.3 %collective-permute-start.7 = (bf16[1056,128]{1,0:T(8,128)(2,1)S(1)}, bf16[1056,128]{1,0:T(8,128)(2,1)S(1)}, u32[]{:S(2)}, u32[]{:S(2)}) collective-permute-start(bf16[1056,128]{1,0:T(8,128)(2,1)S(1)} %concatenate.10.refs_0_), channel_id=1, source_target_pairs={{0,56},{8,0},{16,8},{24,16},{32,24},{40,32},{48,40},{56,48},{64,12... | collective-permute-start | bytes 811016 | tf_op jit(solution)/shard_map/ppermute | solution.py:463
  9.6 17.8 %collective-permute-start.6 = (bf16[1056,128]{1,0:T(8,128)(2,1)S(1)}, bf16[1056,128]{1,0:T(8,128)(2,1)S(1)}, u32[]{:S(2)}, u32[]{:S(2)}) collective-permute-start(bf16[1056,128]{1,0:T(8,128)(2,1)S(1)} %concatenate.10.refs_0_), channel_id=1, source_target_pairs={{0,8},{8,16},{16,24},{24,32},{32,40},{40,48},{48,56},{56,0},{64,72... | collective-permute-start | bytes 811016 | tf_op jit(solution)/shard_map/ppermute | solution.py:463
  27.4 35.4 %collective-permute-start.17 = (bf16[4,256,512]{2,1,0:T(8,128)(2,1)}, bf16[4,256,512]{2,1,0:T(8,128)(2,1)S(1)}, u32[]{:S(2)}, u32[]{:S(2)}) collective-permute-start(bf16[4,256,512]{2,1,0:T(8,128)(2,1)} %get-tuple-element.100), channel_id=1, source_target_pairs={{0,1},{1,0},{2,3},{3,2},{4,5},{5,4},{6,7},{7,6},{8,9},{9,8},{10,11... | collective-permute-start | bytes 3145736 | tf_op jit(solution)/shard_map/ppermute | solution.py:446
  27.4 21.6 %collective-permute-start.10 = (bf16[1056,128]{1,0:T(8,128)(2,1)S(1)}, bf16[1056,128]{1,0:T(8,128)(2,1)S(1)}, u32[]{:S(2)}, u32[]{:S(2)}) collective-permute-start(bf16[1056,128]{1,0:T(8,128)(2,1)S(1)} %collective-permute-done.8.refs_3_), channel_id=1, source_target_pairs={{0,8},{8,16},{16,24},{24,32},{32,40},{40,48},{48,56},{56,0},{64,72... | collective-permute-start | bytes 811016 | tf_op jit(solution)/shard_map/ppermute | solution.py:463
  29.8 16.4 %collective-permute-start.12 = (bf16[528,128]{1,0:T(8,128)(2,1)}, bf16[528,128]{1,0:T(8,128)(2,1)S(1)}, u32[]{:S(2)}, u32[]{:S(2)}) collective-permute-start(bf16[528,128]{1,0:T(8,128)(2,1)} %get-tuple-element.88), channel_id=1, source_target_pairs={{0,16},{8,24},{16,32},{24,40},{32,48},{40,56},{48,0},{56,8},{64,80... | collective-permute-start | bytes 405512 | tf_op jit(solution)/shard_map/ppermute | solution.py:463
  32.8 13.8 %collective-permute-start.13 = (bf16[528,128]{1,0:T(8,128)(2,1)}, bf16[528,128]{1,0:T(8,128)(2,1)S(1)}, u32[]{:S(2)}, u32[]{:S(2)}) collective-permute-start(bf16[528,128]{1,0:T(8,128)(2,1)} %get-tuple-element.89), channel_id=1, source_target_pairs={{0,48},{8,56},{16,0},{24,8},{32,16},{40,24},{48,32},{56,40},{64,11... | collective-permute-start | bytes 405512 | tf_op jit(solution)/shard_map/ppermute | solution.py:463
  35.0 15.5 %collective-permute-start.11 = (bf16[1056,128]{1,0:T(8,128)(2,1)S(1)}, bf16[1056,128]{1,0:T(8,128)(2,1)S(1)}, u32[]{:S(2)}, u32[]{:S(2)}) collective-permute-start(bf16[1056,128]{1,0:T(8,128)(2,1)S(1)} %collective-permute-done.9.refs_4_), channel_id=1, source_target_pairs={{0,56},{8,0},{16,8},{24,16},{32,24},{40,32},{48,40},{56,48},{64,12... | collective-permute-start | bytes 811016 | tf_op jit(solution)/shard_map/ppermute | solution.py:463
  46.1 9.6 %collective-permute-start.14 = (bf16[1056,128]{1,0:T(8,128)(2,1)}, bf16[1056,128]{1,0:T(8,128)(2,1)S(1)}, u32[]{:S(2)}, u32[]{:S(2)}) collective-permute-start(bf16[1056,128]{1,0:T(8,128)(2,1)} %get-tuple-element.90), channel_id=1, source_target_pairs={{0,64},{8,72},{16,80},{24,88},{32,96},{40,104},{48,112},{56,120},{... | collective-permute-start | bytes 811016 | tf_op jit(solution)/shard_map/ppermute | solution.py:468
  46.6 11.3 %collective-permute-start.15 = (bf16[1056,128]{1,0:T(8,128)(2,1)}, bf16[1056,128]{1,0:T(8,128)(2,1)}, u32[]{:S(2)}, u32[]{:S(2)}) collective-permute-start(bf16[1056,128]{1,0:T(8,128)(2,1)} %get-tuple-element.91), channel_id=1, source_target_pairs={{0,128},{8,136},{16,144},{24,152},{32,160},{40,168},{48,176},{56,1... | collective-permute-start | bytes 811016 | tf_op jit(solution)/shard_map/ppermute | solution.py:468
  49.0 13.0 %collective-permute-start.16 = (bf16[1056,128]{1,0:T(8,128)(2,1)}, bf16[1056,128]{1,0:T(8,128)(2,1)}, u32[]{:S(2)}, u32[]{:S(2)}) collective-permute-start(bf16[1056,128]{1,0:T(8,128)(2,1)} %get-tuple-element.92), channel_id=1, source_target_pairs={{0,192},{8,200},{16,208},{24,216},{32,224},{40,232},{48,240},{56,2... | collective-permute-start | bytes 811016 | tf_op jit(solution)/shard_map/ppermute | solution.py:468
  55.7 30.8 %copy-start = (bf16[1056,128]{1,0:T(8,128)(2,1)}, bf16[1056,128]{1,0:T(8,128)(2,1)S(1)}, u32[]{:S(2)}) copy-start(bf16[1056,128]{1,0:T(8,128)(2,1)S(1)} %collective-permute-done.14.refs_9_) | copy-start | bytes 811012
  65.5 9.8 %collective-permute-start.21 = (bf16[256,512]{1,0:T(8,128)(2,1)}, bf16[256,512]{1,0:T(8,128)(2,1)S(1)}, u32[]{:S(2)}, u32[]{:S(2)}) collective-permute-start(bf16[256,512]{1,0:T(8,128)(2,1)} %get-tuple-element.126), channel_id=1, source_target_pairs={{0,2},{1,3},{2,4},{3,5},{4,6},{5,7},{6,0},{7,1},{8,10},{9,11},{10,... | collective-permute-start | bytes 786440 | tf_op jit(solution)/shard_map/ppermute | solution.py:457
  67.2 13.2 %collective-permute-start.23 = (bf16[256,512]{1,0:T(8,128)(2,1)}, bf16[256,512]{1,0:T(8,128)(2,1)S(1)}, u32[]{:S(2)}, u32[]{:S(2)}) collective-permute-start(bf16[256,512]{1,0:T(8,128)(2,1)} %get-tuple-element.127), channel_id=1, source_target_pairs={{0,6},{1,7},{2,0},{3,1},{4,2},{5,3},{6,4},{7,5},{8,14},{9,15},{10,... | collective-permute-start | bytes 786440 | tf_op jit(solution)/shard_map/ppermute | solution.py:457
  68.8 13.3 %collective-permute-start.22 = (bf16[256,512]{1,0:T(8,128)(2,1)}, bf16[256,512]{1,0:T(8,128)(2,1)S(1)}, u32[]{:S(2)}, u32[]{:S(2)}) collective-permute-start(bf16[256,512]{1,0:T(8,128)(2,1)} %get-tuple-element.128), channel_id=1, source_target_pairs={{0,4},{1,5},{2,6},{3,7},{4,0},{5,1},{6,2},{7,3},{8,12},{9,13},{10,... | collective-permute-start | bytes 786440 | tf_op jit(solution)/shard_map/ppermute | solution.py:457
  70.8 13.1 %collective-permute-start.18 = (bf16[1056,128]{1,0:T(8,128)(2,1)}, bf16[1056,128]{1,0:T(8,128)(2,1)S(1)}, u32[]{:S(2)}, u32[]{:S(2)}) collective-permute-start(bf16[1056,128]{1,0:T(8,128)(2,1)} %get-tuple-element.102), channel_id=1, source_target_pairs={{0,64},{8,72},{16,80},{24,88},{32,96},{40,104},{48,112},{56,120},{... | collective-permute-start | bytes 811016 | tf_op jit(solution)/shard_map/ppermute | solution.py:468
  71.8 12.1 %collective-permute-start.19 = (bf16[1056,128]{1,0:T(8,128)(2,1)}, bf16[1056,128]{1,0:T(8,128)(2,1)S(1)}, u32[]{:S(2)}, u32[]{:S(2)}) collective-permute-start(bf16[1056,128]{1,0:T(8,128)(2,1)} %get-tuple-element.103), channel_id=1, source_target_pairs={{0,128},{8,136},{16,144},{24,152},{32,160},{40,168},{48,176},{56,1... | collective-permute-start | bytes 811016 | tf_op jit(solution)/shard_map/ppermute | solution.py:468
  75.3 11.2 %collective-permute-start.20 = (bf16[1056,128]{1,0:T(8,128)(2,1)}, bf16[1056,128]{1,0:T(8,128)(2,1)S(1)}, u32[]{:S(2)}, u32[]{:S(2)}) collective-permute-start(bf16[1056,128]{1,0:T(8,128)(2,1)} %get-tuple-element.104), channel_id=1, source_target_pairs={{0,192},{8,200},{16,208},{24,216},{32,224},{40,232},{48,240},{56,2... | collective-permute-start | bytes 811016 | tf_op jit(solution)/shard_map/ppermute | solution.py:468
  83.9 2.6 %copy-start.1 = (bf16[1056,128]{1,0:T(8,128)(2,1)}, bf16[1056,128]{1,0:T(8,128)(2,1)S(1)}, u32[]{:S(2)}) copy-start(bf16[1056,128]{1,0:T(8,128)(2,1)S(1)} %collective-permute-done.18.refs_12_) | copy-start | bytes 811012
  83.9 2.6 %copy-start.2 = (bf16[1056,128]{1,0:T(8,128)(2,1)}, bf16[1056,128]{1,0:T(8,128)(2,1)S(1)}, u32[]{:S(2)}) copy-start(bf16[1056,128]{1,0:T(8,128)(2,1)S(1)} %collective-permute-done.19.refs_13_) | copy-start | bytes 811012
  86.5 0.7 copy-start.3
  95.6 2.6 %collective-permute-start.24 = (bf16[4,192,512]{2,1,0:T(8,128)(2,1)}, bf16[4,192,512]{2,1,0:T(8,128)(2,1)S(1)}, u32[]{:S(2)}, u32[]{:S(2)}) collective-permute-start(bf16[4,192,512]{2,1,0:T(8,128)(2,1)} %get-tuple-element.122), channel_id=1, source_target_pairs={{0,1},{1,0},{2,3},{3,2},{4,5},{5,4},{6,7},{7,6},{8,9},{9,8},{10,11... | collective-permute-start | bytes 2359304 | tf_op jit(solution)/shard_map/ppermute | solution.py:446
  99.4 8.2 %collective-permute-start.25 = (bf16[192,512]{1,0:T(8,128)(2,1)S(1)}, bf16[192,512]{1,0:T(8,128)(2,1)S(1)}, u32[]{:S(2)}, u32[]{:S(2)}) collective-permute-start(bf16[192,512]{1,0:T(8,128)(2,1)S(1)} %get-tuple-element.129), channel_id=1, source_target_pairs={{0,2},{1,3},{2,4},{3,5},{4,6},{5,7},{6,0},{7,1},{8,10},{9,11},{10,... | collective-permute-start | bytes 589832 | tf_op jit(solution)/shard_map/ppermute | solution.py:457
  99.9 9.4 %collective-permute-start.27 = (bf16[192,512]{1,0:T(8,128)(2,1)S(1)}, bf16[192,512]{1,0:T(8,128)(2,1)S(1)}, u32[]{:S(2)}, u32[]{:S(2)}) collective-permute-start(bf16[192,512]{1,0:T(8,128)(2,1)S(1)} %get-tuple-element.130), channel_id=1, source_target_pairs={{0,6},{1,7},{2,0},{3,1},{4,2},{5,3},{6,4},{7,5},{8,14},{9,15},{10,... | collective-permute-start | bytes 589832 | tf_op jit(solution)/shard_map/ppermute | solution.py:457
  102.7 10.4 %collective-permute-start.26 = (bf16[192,512]{1,0:T(8,128)(2,1)S(1)}, bf16[192,512]{1,0:T(8,128)(2,1)S(1)}, u32[]{:S(2)}, u32[]{:S(2)}) collective-permute-start(bf16[192,512]{1,0:T(8,128)(2,1)S(1)} %get-tuple-element.131), channel_id=1, source_target_pairs={{0,4},{1,5},{2,6},{3,7},{4,0},{5,1},{6,2},{7,3},{8,12},{9,13},{10,... | collective-permute-start | bytes 589832 | tf_op jit(solution)/shard_map/ppermute | solution.py:457
